TPU v7x, 512 devices: a whole 4x4x16 slice. The times are simulated.
512 devices in a mesh: group: 16 (over x_lo, y, core), dp: 32 (over z, x_hi).
Axes of the slice: x: 4 (x_hi: 2, x_lo: 2; x = x_hi * 2 + x_lo), y: 4, z: 16, core: 2. Of those that a mesh axis runs over, the one named last changes fastest.
Arguments:
- table: bfloat16 [262144, 1024], P(('group', 'dp')), may hold values from -6 to 6
- accum: float32 [262144], P(('group', 'dp')), may hold values from 0.05 to 5
- pair_block: int32 [262144], P(('group', 'dp')), may hold values from 0 to 2047, as said below
- pair_protein: int32 [262144], P(('group', 'dp')), may hold values from 0 to 2047, as said below
- pair_weight: bfloat16 [262144, 128], P(('group', 'dp')), may hold values from 0 to 1, as said below
- w_hidden: bfloat16 [1024, 1024], replicated, may hold values from -0.1875 to 0.1875
- hidden_cot: bfloat16 [2048, 1024], P(('group', 'dp')), may hold values from -6 to 6
Outputs:
- new_table: bfloat16 [262144, 1024], P(('group', 'dp'))
- new_accum: float32 [262144], P(('group', 'dp'))
Inputs may be any that keep to these rules, and one draw needn't show every extreme that they name: `pair_block`: the owner of block b is device b // 4 along group+dp. Of one device's 512 pairs at most 2 name blocks of one owner; every device reaches 2 for some owner, and some owner receives 2 pairs from every device. `pair_protein`: A device's pairs name only that device's proteins (index // 4 is the device's index along group+dp), each of them at least once. `pair_weight`: Nonnegative; every pair has at least one positive weight.
All inputs are finite; a program needn't handle non-finite values.
Results may differ from a plain program's by a relative error of at most 0.001.
Values may be sent and summed in bfloat16 or wider, within the bound.
No kernel may reach another device: no remote copies, remote signals or barrier semaphores. Data moves between devices by JAX's collectives and lax.ppermute only.
A program may use at most 64 MiB of HBM per device.

v0:
```python
import jax
import jax.numpy as jnp
from jax import lax
from jax.sharding import PartitionSpec as P

CAP = 2


def mlp_grad(bag, w_hidden, hidden_cot):
    inv = lax.rsqrt(jnp.mean(bag * bag, axis=-1, keepdims=True) + 1e-06)
    unit = bag * inv
    unit_b = unit.astype(jnp.bfloat16)
    pre = jnp.dot(unit_b, w_hidden, preferred_element_type=jnp.float32)
    sig = jax.nn.sigmoid(pre)
    dpre = (hidden_cot.astype(jnp.float32) * sig * (1.0 + pre * (1.0 - sig))).astype(jnp.bfloat16)
    dunit = lax.dot_general(
        dpre, w_hidden, (((1,), (1,)), ((), ())), preferred_element_type=jnp.float32
    )
    dbag = (dunit - unit * jnp.mean(dunit * unit, axis=-1, keepdims=True)) * inv
    return dbag.astype(jnp.bfloat16)


def per_device(table, accum, pair_block, pair_protein, pair_weight, w_hidden, hidden_cot):
    n_group = lax.axis_size("group")
    n_dp = lax.axis_size("dp")
    devices = n_group * n_dp
    rows_dev, width = table.shape
    block_rows = pair_weight.shape[1]
    blocks_dev = rows_dev // block_rows
    pairs = pair_block.shape[0]
    proteins = hidden_cot.shape[0]
    slots = CAP * devices
    device_id = lax.axis_index("group") * n_dp + lax.axis_index("dp")
    owner = pair_block // blocks_dev
    local_block = pair_block % blocks_dev
    local_prot = pair_protein - device_id * proteins
    positions = jnp.arange(pairs, dtype=jnp.int32)
    earlier = (owner[:, None] == owner[None, :]) & (positions[None, :] < positions[:, None])
    rank = jnp.sum(earlier.astype(jnp.int32), axis=1)
    slot = owner * CAP + rank
    place = slot[None, :] == jnp.arange(slots, dtype=jnp.int32)[:, None]
    place_b = place.astype(jnp.bfloat16)
    send_w = jnp.dot(place_b, pair_weight, preferred_element_type=jnp.float32).astype(jnp.bfloat16)
    send_blk = jnp.max(jnp.where(place, local_block[None, :], -1), axis=1)
    send_pid = jnp.max(jnp.where(place, pair_protein[None, :], -1), axis=1)
    got_w, got_blk, got_pid = (
        lax.all_to_all(
            lax.all_to_all(
                send_w.reshape(n_group, n_dp, CAP, block_rows),
                "group",
                split_axis=0,
                concat_axis=0,
                tiled=True,
            ),
            "dp",
            split_axis=1,
            concat_axis=1,
            tiled=True,
        ),
        lax.all_to_all(
            lax.all_to_all(
                send_blk.reshape(n_group, n_dp, CAP),
                "group",
                split_axis=0,
                concat_axis=0,
                tiled=True,
            ),
            "dp",
            split_axis=1,
            concat_axis=1,
            tiled=True,
        ),
        lax.all_to_all(
            lax.all_to_all(
                send_pid.reshape(n_group, n_dp, CAP),
                "group",
                split_axis=0,
                concat_axis=0,
                tiled=True,
            ),
            "dp",
            split_axis=1,
            concat_axis=1,
            tiled=True,
        ),
    )
    got_w = got_w.reshape(slots, block_rows)
    got_blk = got_blk.reshape(slots)
    got_pid = got_pid.reshape(slots)
    hit = got_blk[:, None, None] == jnp.arange(blocks_dev, dtype=jnp.int32)[None, :, None]
    dense = jnp.where(hit, got_w[:, None, :], jnp.zeros((), jnp.bfloat16)).reshape(slots, rows_dev)
    partial_value = jnp.dot(dense, table, preferred_element_type=jnp.float32).astype(jnp.bfloat16)
    returned = lax.all_to_all(
        lax.all_to_all(
            partial_value.reshape(n_group, n_dp, CAP, width),
            "group",
            split_axis=0,
            concat_axis=0,
            tiled=True,
        ),
        "dp",
        split_axis=1,
        concat_axis=1,
        tiled=True,
    )
    returned = returned.reshape(slots, width)
    prot_onehot = (local_prot[None, :] == jnp.arange(proteins, dtype=jnp.int32)[:, None]).astype(
        jnp.bfloat16
    )
    prot_slot = lax.dot_general(
        prot_onehot, place_b, (((1,), (1,)), ((), ())), preferred_element_type=jnp.float32
    ).astype(jnp.bfloat16)
    bag = jnp.dot(prot_slot, returned, preferred_element_type=jnp.float32)
    dbag = mlp_grad(bag, w_hidden, hidden_cot)
    every_grad = lax.all_gather(dbag, ("group", "dp"), axis=0, tiled=True)
    got_grad = jnp.take(every_grad, jnp.maximum(got_pid, 0), axis=0)
    grad = lax.dot_general(
        dense, got_grad, (((0,), (0,)), ((), ())), preferred_element_type=jnp.float32
    )
    acc_new = accum + jnp.mean(grad * grad, axis=-1)
    rows_new = table.astype(jnp.float32) - 0.3 * grad / (jnp.sqrt(acc_new)[:, None] + 1e-08)
    return (rows_new.astype(jnp.bfloat16), acc_new)


def solution(mesh):
    in_specs = (
        P(("group", "dp"), None),
        P(("group", "dp")),
        P(("group", "dp")),
        P(("group", "dp")),
        P(("group", "dp"), None),
        P(),
        P(("group", "dp"), None),
    )
    out_specs = (P(("group", "dp"), None), P(("group", "dp")))
    return jax.shard_map(
        per_device, mesh=mesh, in_specs=in_specs, out_specs=out_specs, check_vma=False
    )
```

profile of v0, /device:TPU:1, one launch (start us, length us, event | category | flops | bytes accessed | tf_op | source)
XLA Modules:
  0.0 1665.0 jit_solution(3884421519699595745)
XLA Ops:
  7.2 0.8 add_select_fusion
  8.3 1.5 select_reduce_fusion
  9.9 0.8 copy.51
  10.7 10.2 all-to-all-start
  20.9 2.1 fusion.5
  22.9 3.8 all-to-all-done
  26.7 3.7 all-to-all-start.2
  30.4 0.7 copy.52
  31.1 6.5 all-to-all-done.2
  37.7 14.1 all-to-all-start.1
  51.7 0.9 copy.54
  52.6 12.9 all-to-all-done.1
  65.5 3.9 all-to-all-start.3
  70.1 18.3 %all-to-all-done.3 = bf16[16,32,2,128]{3,2,0,1:T(2,128)(2,1)S(1)} async-done(((bf16[16,32,2,128]{3,2,0,1:T(2,128)(2,1)}), bf16[16,32,2,128]{3,2,0,1:T(2,128)(2,1)S(1)}, u32[]{:S(2)}, u32[]{:S(2)}) %all-to-all-start.3) | async-done | bytes 262176 | tf_op jit(solution)/shard_map/all_to_all | solution.py:47
  88.7 5.1 broadcast_select_fusion
  93.8 3.8 convolution_convert_fusion
  97.6 4.1 reshape.99
  101.7 34.1 %all_to_all.40 = bf16[16,32,2,1024]{3,2,1,0:T(2,128)(2,1)S(1)} all-to-all(bf16[16,32,2,1024]{3,2,1,0:T(2,128)(2,1)} %reshape.99), channel_id=1, replica_groups=mesh['group'=16,'dp'=32] {'group'}, dimensions={0} | all-to-all | bytes 4194304 | tf_op jit(solution)/shard_map/all_to_all | solution.py:94
  135.8 3.5 copy.60
  139.3 4.9 all-to-all-start.7
  144.5 95.5 %all-to-all-done.7 = bf16[16,32,2,1024]{3,2,0,1:T(2,128)(2,1)} async-done(((bf16[16,32,2,1024]{3,2,0,1:T(2,128)(2,1)}), bf16[16,32,2,1024]{3,2,0,1:T(2,128)(2,1)}, u32[]{:S(2)}, u32[]{:S(2)}) %all-to-all-start.7) | async-done | bytes 2097184 | tf_op jit(solution)/shard_map/all_to_all | solution.py:93
  240.0 4.8 copy.61
  244.8 4.1 reshape.100
  248.9 2.4 multiply_reduce_fusion.2
  251.4 1.1 multiply_reduce_fusion.1
  253.6 10.8 all_to_all.41
  264.5 22.6 %all_to_all.42 = s32[16,32,2]{0,2,1:T(2,128)S(1)} all-to-all(s32[16,32,2]{0,2,1:T(2,128)S(1)} %copy.57), channel_id=1, replica_groups=mesh['group'=16,'dp'=32] {'dp'}, dimensions={1} | all-to-all | bytes 8192 | tf_op jit(solution)/shard_map/all_to_all | solution.py:73
  287.9 1349.4 %all-gather.3.cloned.1.call-done = bf16[512,4,1024]{2,1,0:T(4,128)(2,1)} async-done(((bf16[1,4,1024]{2,1,0:T(4,128)(2,1)}), bf16[512,4,1024]{2,1,0:T(4,128)(2,1)}) %all-gather.3.cloned.1.call-update) | async-done | bytes 4194320 | tf_op jit(solution)/shard_map/all_gather | solution.py:115
  1637.3 6.9 reshape.111
  1644.1 8.8 gather_fusion
  1652.9 3.1 multiply_reduce_fusion
  1656.6 1.6 subtract_convert_fusion
  (35 shorter events, 4.2 us)
Async XLA Ops:
  7.2 244.2 %copy-start = (bf16[1024,1024]{1,0:T(8,128)(2,1)S(1)}, bf16[1024,1024]{1,0:T(8,128)(2,1)}, u32[]{:S(2)}) copy-start(bf16[1024,1024]{1,0:T(8,128)(2,1)} %param.12) | copy-start | bytes 6291460
  10.7 16.0 all-to-all-start
  26.7 11.0 all-to-all-start.2
  37.7 27.8 %all-to-all-start.1 = ((s32[16,32,2]{0,2,1:T(2,128)}), s32[16,32,2]{0,2,1:T(2,128)S(1)}, u32[]{:S(2)}, u32[]{:S(2)}) async-start(s32[16,32,2]{0,2,1:T(2,128)} %copy.52), calls=%async_computation.1 | async-start | bytes 65536 | tf_op jit(solution)/shard_map/all_to_all | solution.py:60
  65.5 22.9 %all-to-all-start.3 = ((bf16[16,32,2,128]{3,2,0,1:T(2,128)(2,1)}), bf16[16,32,2,128]{3,2,0,1:T(2,128)(2,1)S(1)}, u32[]{:S(2)}, u32[]{:S(2)}) async-start(bf16[16,32,2,128]{3,2,0,1:T(2,128)(2,1)} %copy.54), calls=%async_computation.3 | async-start | bytes 524288 | tf_op jit(solution)/shard_map/all_to_all | solution.py:47
  139.3 5.2 copy-start.3
  139.3 100.6 %all-to-all-start.7 = ((bf16[16,32,2,1024]{3,2,0,1:T(2,128)(2,1)}), bf16[16,32,2,1024]{3,2,0,1:T(2,128)(2,1)}, u32[]{:S(2)}, u32[]{:S(2)}) async-start(bf16[16,32,2,1024]{3,2,0,1:T(2,128)(2,1)} %copy.60), calls=%async_computation.7 | async-start | bytes 4194304 | tf_op jit(solution)/shard_map/all_to_all | solution.py:93
  144.3 1493.0 %all-gather.3.cloned.1.call-start = ((), (), s32[]{:S(2)}) async-start(), calls=%async_computation.8 | async-start | bytes 4202496 | tf_op jit(solution)/shard_map/all_gather | solution.py:115
  248.9 2.5 copy-start.2
  1652.9 3.1 copy-start.4
  1652.9 3.7 copy-start.1
Sparse Core Ops, SparseCore 0:
  253.3 1383.8 all-gather.2
where the time goes:
time: 1670 us
  waiting for transfers between devices  1490 us (89%)
  blocking collectives  67.4 us (4%)
  starting transfers between devices  36.9 us (2%)
  local copies, waits for them, and re-layouts  36.8 us (2%)
    all_gather x1, waiting for transfers between devices, per_device(): every_grad = lax.all_gather(dbag, ('group', 'dp'), axis=0, tiled=True)  1350 us
    all_to_all x1, waiting for transfers between devices, per_device(): lax.all_to_all(lax.all_to_all(partial_value.reshape(n_group, n_dp, CAP, w...  95.5 us
    all_to_all x1, blocking collectives, per_device(): lax.all_to_all(partial_value.reshape(n_group, n_dp, CAP, width), 'group',...  34.1 us
  transfers between devices with their start and end apart: 6, of which 6 were waited for; matrix products, arithmetic and copies ran while one was open for 0% of the time, Pallas kernels for 0%

commit v1 on v0

v1 whole, which is shorter than its diff:
```python
import jax
import jax.numpy as jnp
from jax import lax
from jax.sharding import Mesh
from jax.sharding import PartitionSpec as P

CAP = 2
AXES = ("xl", "y", "c", "z", "xh")
SIZES = (2, 4, 2, 16, 2)
PLANE = ("xl", "y", "c", "xh")


def mlp_grad(bag, w_hidden, hidden_cot):
    inv = lax.rsqrt(jnp.mean(bag * bag, axis=-1, keepdims=True) + 1e-06)
    unit = bag * inv
    unit_b = unit.astype(jnp.bfloat16)
    pre = jnp.dot(unit_b, w_hidden, preferred_element_type=jnp.float32)
    sig = jax.nn.sigmoid(pre)
    dpre = (hidden_cot.astype(jnp.float32) * sig * (1.0 + pre * (1.0 - sig))).astype(jnp.bfloat16)
    dunit = lax.dot_general(
        dpre, w_hidden, (((1,), (1,)), ((), ())), preferred_element_type=jnp.float32
    )
    dbag = (dunit - unit * jnp.mean(dunit * unit, axis=-1, keepdims=True)) * inv
    return dbag.astype(jnp.bfloat16)


def exchange(x, axes):
    return lax.all_to_all(x, axes, split_axis=0, concat_axis=0, tiled=True)


def per_device(table, accum, pair_block, pair_protein, pair_weight, w_hidden, hidden_cot):
    nz = lax.axis_size("z")
    nh = lax.axis_size("xh")
    devices = lax.axis_size(AXES)
    npl = devices // nz
    n_dp = nz * nh
    rows_dev, width = table.shape
    block_rows = pair_weight.shape[1]
    blocks_dev = rows_dev // block_rows
    pairs = pair_block.shape[0]
    proteins = hidden_cot.shape[0]
    slots = CAP * devices
    device_id = lax.axis_index(AXES)

    owner = pair_block // blocks_dev
    local_block = pair_block % blocks_dev
    local_prot = pair_protein - device_id * proteins
    positions = jnp.arange(pairs, dtype=jnp.int32)
    earlier = (owner[:, None] == owner[None, :]) & (positions[None, :] < positions[:, None])
    rank = jnp.sum(earlier.astype(jnp.int32), axis=1)
    oz = (owner % n_dp) // nh
    opl = (owner // n_dp) * nh + owner % nh
    slot = (oz * npl + opl) * CAP + rank
    code = local_prot * blocks_dev + local_block + 1
    place = slot[None, :] == jnp.arange(slots, dtype=jnp.int32)[:, None]
    send_w = jnp.dot(
        place.astype(jnp.bfloat16), pair_weight, preferred_element_type=jnp.float32
    ).astype(jnp.bfloat16)
    send_code = jnp.max(jnp.where(place, code[None, :], 0), axis=1)

    per_z = npl * CAP
    code_rows = jnp.pad(
        send_code.reshape(nz, 1, per_z).astype(jnp.bfloat16),
        ((0, 0), (0, 7), (0, block_rows - per_z)),
    )
    got1 = exchange(
        jnp.concatenate([send_w.reshape(nz, per_z, block_rows), code_rows], axis=1), "z"
    )
    w1 = got1[:, :per_z].reshape(nz, npl, CAP, block_rows)
    code1 = got1[:, per_z, :per_z].astype(jnp.int32).reshape(nz, npl, CAP)
    code1 = code1.transpose(1, 0, 2) - 1
    w1 = w1.transpose(1, 0, 2, 3)

    per_p = nz * CAP
    blk1 = (code1 & (blocks_dev - 1)).astype(jnp.bfloat16)
    blk_rows = jnp.pad(
        blk1.reshape(npl, 1, per_p), ((0, 0), (0, 7), (0, block_rows - per_p))
    )
    got2 = exchange(
        jnp.concatenate([w1.reshape(npl, per_p, block_rows), blk_rows], axis=1), PLANE
    )
    w2 = got2[:, :per_p].reshape(slots, block_rows)
    blk2 = got2[:, per_p, :per_p].astype(jnp.int32).reshape(slots)
    hit = blk2[:, None, None] == jnp.arange(blocks_dev, dtype=jnp.int32)[None, :, None]
    dense = jnp.where(hit, w2[:, None, :], jnp.zeros((), jnp.bfloat16)).reshape(slots, rows_dev)
    partial_value = jnp.dot(dense, table, preferred_element_type=jnp.float32).astype(jnp.bfloat16)

    got3 = exchange(partial_value.reshape(npl, per_p, width), PLANE).reshape(slots, width)
    prot1 = lax.shift_right_arithmetic(code1, blocks_dev.bit_length() - 1)
    zs = jnp.arange(nz, dtype=jnp.int32)
    target = prot1 + jnp.where(prot1 >= 0, zs[None, :, None] * proteins, 0)
    member = (
        target.reshape(1, slots) == jnp.arange(nz * proteins, dtype=jnp.int32)[:, None]
    ).astype(jnp.bfloat16)
    bag_part = jnp.dot(member, got3, preferred_element_type=jnp.float32)
    bag = jnp.sum(exchange(bag_part.reshape(nz, proteins, width), "z"), axis=0)

    dbag = mlp_grad(bag, w_hidden, hidden_cot)

    every = exchange(jnp.broadcast_to(dbag[None], (nz, proteins, width)), "z")
    every = every.reshape(nz * proteins, width)
    send_g = lax.dot_general(
        member, every, (((0,), (0,)), ((), ())), preferred_element_type=jnp.float32
    ).astype(jnp.bfloat16)
    got_grad = exchange(send_g.reshape(npl, per_p, width), PLANE).reshape(slots, width)
    grad = lax.dot_general(
        dense, got_grad, (((0,), (0,)), ((), ())), preferred_element_type=jnp.float32
    )
    acc_new = accum + jnp.mean(grad * grad, axis=-1)
    rows_new = table.astype(jnp.float32) - 0.3 * grad / (jnp.sqrt(acc_new)[:, None] + 1e-08)
    return (rows_new.astype(jnp.bfloat16), acc_new)


def solution(mesh):
    split = Mesh(mesh.devices.reshape(SIZES), AXES)
    in_specs = (
        P(AXES, None),
        P(AXES),
        P(AXES),
        P(AXES),
        P(AXES, None),
        P(),
        P(AXES, None),
    )
    out_specs = (P(AXES, None), P(AXES))
    return jax.shard_map(
        per_device, mesh=split, in_specs=in_specs, out_specs=out_specs, check_vma=False
    )
```

time: 1670 us -> 185 us (0.11)
  waiting for transfers between devices: 1490 us -> 27.9 us
  blocking collectives: 67.4 us -> 129 us
  local copies, waits for them, and re-layouts: 36.8 us -> 1.66 us
  starting transfers between devices: 36.9 us -> 4.7 us
    all_gather x1 -> x0, waiting for transfers between devices: 1350 us -> none  [per_device(): every_grad = lax.all_gather(dbag, ('group', 'dp'), axis=0, tiled=True)]
    all_to_all x5 -> x1, waiting for transfers between devices: 137 us -> 27.9 us  [exchange(): return lax.all_to_all(x, axes, split_axis=0, concat_axis=0, tiled=True)]
    all_to_all x3 -> x5, blocking collectives: 67.4 us -> 129 us  [exchange(): return lax.all_to_all(x, axes, split_axis=0, concat_axis=0, tiled=True)]
    all_to_all x5 -> x1, starting transfers between devices: 36.7 us -> 4.7 us  [exchange(): return lax.all_to_all(x, axes, split_axis=0, concat_axis=0, tiled=True)]
  transfers between devices with their start and end apart: 6 -> 1, of which waited for: 6 -> 1; matrix products, arithmetic and copies ran while one was open for 0% -> 0% of each run, Pallas kernels for 0% -> 0%
where the time goes in v1:
time: 185 us; the launch traced here: 184 us
  blocking collectives  129 us (70%)
  waiting for transfers between devices  27.9 us (15%)
  matrix products  10.5 us (6%)
  other arithmetic  9.38 us (5%)
  starting transfers between devices  4.7 us (3%)
    all_to_all x5, blocking collectives, exchange(): return lax.all_to_all(x, axes, split_axis=0, concat_axis=0, tiled=True)  129 us
    all_to_all x1, waiting for transfers between devices, exchange(): return lax.all_to_all(x, axes, split_axis=0, concat_axis=0, tiled=True)  27.9 us
    select_n x1, other arithmetic, per_device(): jnp.where(hit, w2[:, None, :], jnp.zeros((), jnp.bfloat16))  5.11 us
    all_to_all x1, starting transfers between devices, exchange(): return lax.all_to_all(x, axes, split_axis=0, concat_axis=0, tiled=True)  4.7 us
    dot_general x1, matrix products, per_device(): jnp.dot(dense, table, preferred_element_type=jnp.float32)  3.78 us
  transfers between devices with their start and end apart: 1, of which 1 were waited for; matrix products, arithmetic and copies ran while one was open for 0% of the time, Pallas kernels for 0%

profile of v1, /device:TPU:1, one launch (start us, length us, event | category | flops | bytes accessed | tf_op | source)
XLA Modules:
  0.0 184.1 jit_solution(15274843379722978987)
XLA Ops:
  0.7 0.9 add_select_fusion.5
  1.5 0.2 convert_reduce_fusion
  1.8 0.4 select_reduce_fusion
  2.2 1.4 fusion.1
  3.7 29.3 %all_to_all.30 = bf16[16,72,128]{2,1,0:T(8,128)(2,1)S(1)} all-to-all(bf16[16,72,128]{2,1,0:T(8,128)(2,1)S(1)} %fusion.12), channel_id=1, replica_groups=mesh['xl'=2,'y'=4,'c'=2,'z'=16,'xh'=2] {'z'}, dimensions={0} | all-to-all | bytes 589824 | tf_op jit(solution)/shard_map/all_to_all | solution.py:28
  33.0 0.2 copy.53
  33.2 0.1 copy.44
  33.3 0.1 copy.46
  33.4 0.1 copy.47
  33.5 0.1 copy.48
  33.6 0.1 copy.49
  33.8 22.8 %all_to_all.31 = bf16[32,40,128]{2,1,0:T(8,128)(2,1)S(1)} all-to-all(bf16[32,40,128]{2,1,0:T(8,128)(2,1)S(1)} %copy.49), channel_id=1, replica_groups=mesh['xl'=2,'y'=4,'c'=2,'z'=16,'xh'=2] {'xl','y','c','xh'}, dimensions={0} | all-to-all | bytes 655360 | tf_op jit(solution)/shard_map/all_to_all | solution.py:28
  56.7 0.2 iota_compare_fusion.7
  56.9 5.1 %broadcast_select_fusion = bf16[1024,4,128]{2,1,0:T(4,128)(2,1)S(1)} fusion(pred[1024,4]{1,0:T(8,128)(4,1)S(1)} %iota_compare_fusion.7, bf16[1024,128]{1,0:T(8,128)(2,1)S(1)} %bitcast.41), kind=kLoop, calls=%fused_computation.15 | loop fusion | flops 524288 | bytes 1314816 | tf_op jit(solution)/shard_map/jit(_where)/select_n | solution.py:85
  62.1 3.8 %convolution_convert_fusion.1 = bf16[1024,1024]{1,0:T(8,128)(2,1)} fusion(bf16[512,1024]{1,0:T(8,128)(2,1)} %param.7, bf16[128,8,4,128]{3,2,1,0:T(4,128)(2,1)S(1)} %bitcast.36), kind=kOutput, calls=%fused_computation.6 | convolution fusion | flops 1074790400 | bytes 4194304 | tf_op jit(solution)/shard_map/dot_general | solution.py:86
  65.8 4.7 %all-to-all-start.2 = ((bf16[32,32,1024]{2,1,0:T(8,128)(2,1)}), bf16[32,32,1024]{2,1,0:T(8,128)(2,1)}, u32[]{:S(2)}, u32[]{:S(2)}) async-start(bf16[32,32,1024]{2,1,0:T(8,128)(2,1)} %bitcast.38), calls=%async_computation.2 | async-start | bytes 4194304 | tf_op jit(solution)/shard_map/all_to_all | solution.py:28
  70.6 0.1 copy.50
  70.7 0.3 copy.51
  71.0 0.2 eq.89
  71.1 27.9 %all-to-all-done.2 = bf16[32,32,1024]{2,1,0:T(8,128)(2,1)} async-done(((bf16[32,32,1024]{2,1,0:T(8,128)(2,1)}), bf16[32,32,1024]{2,1,0:T(8,128)(2,1)}, u32[]{:S(2)}, u32[]{:S(2)}) %all-to-all-start.2) | async-done | bytes 2097184 | tf_op jit(solution)/shard_map/all_to_all | solution.py:28
  99.0 2.1 %fusion.13 = f32[16,4,1024]{2,0,1:T(8,128)S(1)} fusion(bf16[1024,1024,1]{1,0,2:T(8,128)(2,1)} %bitcast.13, s32[16,4]{0,1:T(4,128)S(1)} %multiply_add_fusion.1, s32[1024]{0:T(1024)S(1)} %eq.89), kind=kOutput, calls=%fused_computation.26 | convolution fusion | flops 134283264 | bytes 2363648 | tf_op jit(solution)/shard_map/dot_general | solution.py:95
  101.1 0.2 copy.52
  101.3 18.9 %all_to_all.32 = f32[16,4,1024]{2,1,0:T(4,128)S(1)} all-to-all(f32[16,4,1024]{2,1,0:T(4,128)S(1)} %copy.52), channel_id=1, replica_groups=mesh['xl'=2,'y'=4,'c'=2,'z'=16,'xh'=2] {'z'}, dimensions={0} | all-to-all | bytes 524288 | tf_op jit(solution)/shard_map/all_to_all | solution.py:28
  120.3 0.1 multiply_reduce_fusion.2
  120.5 1.1 multiply_reduce_fusion.1
  121.5 0.1 multiply_convert_fusion
  121.7 22.7 %all_to_all.33 = bf16[16,4,1024]{2,1,0:T(4,128)(2,1)S(1)} all-to-all(bf16[16,4,1024]{2,1,0:T(4,128)(2,1)S(1)} %broadcast_in_dim.70), channel_id=1, replica_groups=mesh['xl'=2,'y'=4,'c'=2,'z'=16,'xh'=2] {'z'}, dimensions={0} | all-to-all | bytes 262144 | tf_op jit(solution)/shard_map/all_to_all | solution.py:28
  144.4 0.8 convolution_convert_fusion
  145.2 35.4 %all_to_all.34 = bf16[32,32,1024]{2,1,0:T(8,128)(2,1)S(1)} all-to-all(bf16[32,32,1024]{2,1,0:T(8,128)(2,1)S(1)} %bitcast.35), channel_id=1, replica_groups=mesh['xl'=2,'y'=4,'c'=2,'z'=16,'xh'=2] {'xl','y','c','xh'}, dimensions={0} | all-to-all | bytes 4194304 | tf_op jit(solution)/shard_map/all_to_all | solution.py:28
  180.6 1.4 multiply_reduce_fusion
  182.0 0.6 sqrt_add_fusion
  182.6 1.6 subtract_convert_fusion
  (27 shorter events, 0.6 us)
Async XLA Ops:
  0.6 119.8 %copy-start = (bf16[1024,1024]{1,0:T(8,128)(2,1)S(1)}, bf16[1024,1024]{1,0:T(8,128)(2,1)}, u32[]{:S(2)}) copy-start(bf16[1024,1024]{1,0:T(8,128)(2,1)} %param.12) | copy-start | bytes 6291460
  65.8 33.2 %all-to-all-start.2 = ((bf16[32,32,1024]{2,1,0:T(8,128)(2,1)}), bf16[32,32,1024]{2,1,0:T(8,128)(2,1)}, u32[]{:S(2)}, u32[]{:S(2)}) async-start(bf16[32,32,1024]{2,1,0:T(8,128)(2,1)} %bitcast.38), calls=%async_computation.2 | async-start | bytes 4194304 | tf_op jit(solution)/shard_map/all_to_all | solution.py:28
  70.7 49.8 %copy-start.2 = (bf16[4,1024]{1,0:T(4,128)(2,1)S(1)}, bf16[4,1024]{1,0:T(4,128)(2,1)}, u32[]{:S(2)}) copy-start(bf16[4,1024]{1,0:T(4,128)(2,1)} %param.13) | copy-start | bytes 24580
  180.6 1.4 copy-start.3
  180.6 2.0 %copy-start.1 = (bf16[512,1024]{1,0:T(8,128)(2,1)S(1)}, bf16[512,1024]{1,0:T(8,128)(2,1)}, u32[]{:S(2)}) copy-start(bf16[512,1024]{1,0:T(8,128)(2,1)} %param.7) | copy-start | bytes 3145732

commit v2 on v1

--- a/solution.py
+++ b/solution.py
@@ -1,6 +1,8 @@
 import jax
 import jax.numpy as jnp
 from jax import lax
+from jax.experimental import pallas as pl
+from jax.experimental.pallas import tpu as pltpu
 from jax.sharding import Mesh
 from jax.sharding import PartitionSpec as P
 
@@ -22,6 +24,55 @@
     )
     dbag = (dunit - unit * jnp.mean(dunit * unit, axis=-1, keepdims=True)) * inv
     return dbag.astype(jnp.bfloat16)
+
+
+def owner_kernel(got_ref, table_ref, partial_ref, dense_ref):
+    groups, _, block_rows = got_ref.shape
+    per_p = partial_ref.shape[1]
+    blocks_dev = table_ref.shape[0] // block_rows
+    width = table_ref.shape[1]
+    got = got_ref[...].astype(jnp.float32)
+    row = got[:, per_p : per_p + 1, :]
+    shape = (groups, per_p, block_rows)
+    diagonal = lax.broadcasted_iota(jnp.int32, shape, 1) == lax.broadcasted_iota(
+        jnp.int32, shape, 2
+    )
+    block = jnp.sum(jnp.where(diagonal, row, 0.0), axis=2, keepdims=True)
+    weights = got[:, :per_p, :]
+    for b in range(blocks_dev):
+        mine = jnp.where(block == b, weights, 0.0).astype(jnp.bfloat16)
+        dense_ref[:, b * block_rows : (b + 1) * block_rows] = mine.reshape(
+            groups * per_p, block_rows
+        )
+    partial_ref[...] = (
+        jnp.dot(dense_ref[...], table_ref[...], preferred_element_type=jnp.float32)
+        .astype(jnp.bfloat16)
+        .reshape(groups, per_p, width)
+    )
+
+
+def owner_partials(got, table, per_p):
+    npl, rows, block_rows = got.shape
+    rows_dev, width = table.shape
+    step = 8
+    return pl.pallas_call(
+        owner_kernel,
+        grid=(npl // step,),
+        in_specs=[
+            pl.BlockSpec((step, rows, block_rows), lambda i: (i, 0, 0)),
+            pl.BlockSpec((rows_dev, width), lambda i: (0, 0)),
+        ],
+        out_specs=[
+            pl.BlockSpec((step, per_p, width), lambda i: (i, 0, 0)),
+            pl.BlockSpec((step * per_p, rows_dev), lambda i: (i, 0)),
+        ],
+        out_shape=[
+            jax.ShapeDtypeStruct((npl, per_p, width), jnp.bfloat16),
+            jax.ShapeDtypeStruct((npl * per_p, rows_dev), jnp.bfloat16),
+        ],
+        compiler_params=pltpu.CompilerParams(vmem_limit_bytes=24 * 2**20),
+        name="owner_partials",
+    )(got, table)
 
 
 def exchange(x, axes):
@@ -79,13 +130,9 @@
     got2 = exchange(
         jnp.concatenate([w1.reshape(npl, per_p, block_rows), blk_rows], axis=1), PLANE
     )
-    w2 = got2[:, :per_p].reshape(slots, block_rows)
-    blk2 = got2[:, per_p, :per_p].astype(jnp.int32).reshape(slots)
-    hit = blk2[:, None, None] == jnp.arange(blocks_dev, dtype=jnp.int32)[None, :, None]
-    dense = jnp.where(hit, w2[:, None, :], jnp.zeros((), jnp.bfloat16)).reshape(slots, rows_dev)
-    partial_value = jnp.dot(dense, table, preferred_element_type=jnp.float32).astype(jnp.bfloat16)
+    partial_value, dense = owner_partials(got2, table, per_p)
 
-    got3 = exchange(partial_value.reshape(npl, per_p, width), PLANE).reshape(slots, width)
+    got3 = exchange(partial_value, PLANE).reshape(slots, width)
     prot1 = lax.shift_right_arithmetic(code1, blocks_dev.bit_length() - 1)
     zs = jnp.arange(nz, dtype=jnp.int32)
     target = prot1 + jnp.where(prot1 >= 0, zs[None, :, None] * proteins, 0)

time: 185 us -> 180 us (0.973)
  other arithmetic: 9.38 us -> 4.02 us
  matrix products: 10.5 us -> 6.66 us
  local copies, waits for them, and re-layouts: 1.66 us -> 3.81 us
  Pallas kernels: 0 us -> 2.04 us
    select_n x1 -> x0, other arithmetic: 5.11 us -> none  [per_device(): jnp.where(hit, w2[:, None, :], jnp.zeros((), jnp.bfloat16))]
    dot_general x1 -> x0, matrix products: 3.78 us -> none  [per_device(): jnp.dot(dense, table, preferred_element_type=jnp.float32)]
    unnamed x9 -> x15, local copies, waits for them, and re-layouts: 0.2 us -> 2.46 us
    pallas_call x0 -> x1, Pallas kernels: none -> 2.04 us  [owner_partials(): pl.pallas_call(owner_kernel, grid=(npl // step,), in_specs=[pl.BlockSpec(...]
where the time goes in v2:
time: 180 us; the launch traced here: 179 us
  blocking collectives  129 us (72%)
  waiting for transfers between devices  27.9 us (16%)
  matrix products  6.66 us (4%)
  starting transfers between devices  4.71 us (3%)
  other arithmetic  4.02 us (2%)
  local copies, waits for them, and re-layouts  3.81 us (2%)
  Pallas kernels  2.04 us (1%)
    all_to_all x5, blocking collectives, exchange(): return lax.all_to_all(x, axes, split_axis=0, concat_axis=0, tiled=True)  129 us
    all_to_all x1, waiting for transfers between devices, exchange(): return lax.all_to_all(x, axes, split_axis=0, concat_axis=0, tiled=True)  27.9 us
    all_to_all x1, starting transfers between devices, exchange(): return lax.all_to_all(x, axes, split_axis=0, concat_axis=0, tiled=True)  4.71 us
  transfers between devices with their start and end apart: 1, of which 1 were waited for; matrix products, arithmetic and copies ran while one was open for 0% of the time, Pallas kernels for 0%

profile of v2, /device:TPU:1, one launch (start us, length us, event | category | flops | bytes accessed | tf_op | source)
XLA Modules:
  0.0 179.5 jit_solution(1760354197532100732)
XLA Ops:
  0.7 0.9 add_select_fusion.5
  1.5 0.2 convert_reduce_fusion
  1.8 0.4 select_reduce_fusion
  2.2 0.1 convert_element_type.76
  2.2 1.4 fusion.1
  3.7 29.4 %all_to_all.30 = bf16[16,72,128]{2,1,0:T(8,128)(2,1)S(1)} all-to-all(bf16[16,72,128]{2,1,0:T(8,128)(2,1)S(1)} %fusion.7), channel_id=1, replica_groups=mesh['xl'=2,'y'=4,'c'=2,'z'=16,'xh'=2] {'z'}, dimensions={0} | all-to-all | bytes 589824 | tf_op jit(solution)/shard_map/all_to_all | solution.py:79
  33.1 0.2 copy.44
  33.3 0.2 copy.36
  33.6 0.1 copy.38
  33.7 0.1 copy.39
  33.7 0.1 copy.40
  33.9 22.8 %all_to_all.31.got_ref = bf16[32,40,128]{2,1,0:T(8,128)(2,1)S(1)} all-to-all(bf16[32,40,128]{2,1,0:T(8,128)(2,1)S(1)} %fusion.6), channel_id=1, replica_groups=mesh['xl'=2,'y'=4,'c'=2,'z'=16,'xh'=2] {'xl','y','c','xh'}, dimensions={0} | all-to-all | bytes 655360 | tf_op jit(solution)/shard_map/all_to_all | solution.py:79
  56.7 2.0 %owner_partials.1 = (bf16[32,32,1024]{2,1,0:T(8,128)(2,1)S(1)}, bf16[1024,512]{1,0:T(8,128)(2,1)S(1)}) custom-call(bf16[32,40,128]{2,1,0:T(8,128)(2,1)S(1)} %all_to_all.31.got_ref, bf16[512,1024]{1,0:T(8,128)(2,1)S(1)} %copy-done.1), custom_call_target="tpu_custom_call" | custom-call | tf_op jit(solution)/shard_map/owner_partials/pallas_call | solution.py:58
  58.8 1.3 copy-done.2
  60.0 1.0 copy-done.3
  61.0 4.7 %all-to-all-start.2 = ((bf16[32,32,1024]{2,1,0:T(8,128)(2,1)}), bf16[32,32,1024]{2,1,0:T(8,128)(2,1)}, u32[]{:S(2)}, u32[]{:S(2)}) async-start(bf16[32,32,1024]{2,1,0:T(8,128)(2,1)} %copy-done.2), calls=%async_computation.2 | async-start | bytes 4194304 | tf_op jit(solution)/shard_map/all_to_all | solution.py:79
  65.8 0.1 copy.41
  65.9 0.3 copy.42
  66.1 0.2 eq.68
  66.3 27.9 %all-to-all-done.2 = bf16[32,32,1024]{2,1,0:T(8,128)(2,1)} async-done(((bf16[32,32,1024]{2,1,0:T(8,128)(2,1)}), bf16[32,32,1024]{2,1,0:T(8,128)(2,1)}, u32[]{:S(2)}, u32[]{:S(2)}) %all-to-all-start.2) | async-done | bytes 2097184 | tf_op jit(solution)/shard_map/all_to_all | solution.py:79
  94.2 2.1 %fusion.8 = f32[16,4,1024]{2,0,1:T(8,128)S(1)} fusion(bf16[1024,1024,1]{1,0,2:T(8,128)(2,1)} %bitcast.11, s32[16,4]{0,1:T(4,128)S(1)} %multiply_add_fusion.1, s32[1024]{0:T(1024)S(1)} %eq.68), kind=kOutput, calls=%fused_computation.18 | convolution fusion | flops 134283264 | bytes 2363648 | tf_op jit(solution)/shard_map/dot_general | solution.py:142
  96.3 0.2 copy.43
  96.5 18.9 %all_to_all.32 = f32[16,4,1024]{2,1,0:T(4,128)S(1)} all-to-all(f32[16,4,1024]{2,1,0:T(4,128)S(1)} %copy.43), channel_id=1, replica_groups=mesh['xl'=2,'y'=4,'c'=2,'z'=16,'xh'=2] {'z'}, dimensions={0} | all-to-all | bytes 524288 | tf_op jit(solution)/shard_map/all_to_all | solution.py:79
  115.5 0.1 multiply_reduce_fusion.2
  115.6 1.1 multiply_reduce_fusion.1
  116.7 0.1 multiply_convert_fusion
  116.8 22.7 %all_to_all.33 = bf16[16,4,1024]{2,1,0:T(4,128)(2,1)S(1)} all-to-all(bf16[16,4,1024]{2,1,0:T(4,128)(2,1)S(1)} %broadcast_in_dim.27), channel_id=1, replica_groups=mesh['xl'=2,'y'=4,'c'=2,'z'=16,'xh'=2] {'z'}, dimensions={0} | all-to-all | bytes 262144 | tf_op jit(solution)/shard_map/all_to_all | solution.py:79
  139.6 0.8 convolution_convert_fusion
  140.4 35.5 %all_to_all.34 = bf16[32,32,1024]{2,1,0:T(8,128)(2,1)S(1)} all-to-all(bf16[32,32,1024]{2,1,0:T(8,128)(2,1)S(1)} %bitcast.25), channel_id=1, replica_groups=mesh['xl'=2,'y'=4,'c'=2,'z'=16,'xh'=2] {'xl','y','c','xh'}, dimensions={0} | all-to-all | bytes 4194304 | tf_op jit(solution)/shard_map/all_to_all | solution.py:79
  175.9 1.4 multiply_reduce_fusion
  177.3 0.6 sqrt_add_fusion
  177.9 1.6 subtract_convert_fusion
  (27 shorter events, 0.3 us)
Async XLA Ops:
  0.6 115.0 %copy-start = (bf16[1024,1024]{1,0:T(8,128)(2,1)S(1)}, bf16[1024,1024]{1,0:T(8,128)(2,1)}, u32[]{:S(2)}) copy-start(bf16[1024,1024]{1,0:T(8,128)(2,1)} %param.12) | copy-start | bytes 6291460
  3.6 53.1 %copy-start.1 = (bf16[512,1024]{1,0:T(8,128)(2,1)S(1)}, bf16[512,1024]{1,0:T(8,128)(2,1)}, u32[]{:S(2)}) copy-start(bf16[512,1024]{1,0:T(8,128)(2,1)} %table_ref.1) | copy-start | bytes 3145732
  58.7 1.3 copy-start.2
  60.0 1.0 copy-start.3
  61.0 33.2 %all-to-all-start.2 = ((bf16[32,32,1024]{2,1,0:T(8,128)(2,1)}), bf16[32,32,1024]{2,1,0:T(8,128)(2,1)}, u32[]{:S(2)}, u32[]{:S(2)}) async-start(bf16[32,32,1024]{2,1,0:T(8,128)(2,1)} %copy-done.2), calls=%async_computation.2 | async-start | bytes 4194304 | tf_op jit(solution)/shard_map/all_to_all | solution.py:79
  65.9 49.8 %copy-start.5 = (bf16[4,1024]{1,0:T(4,128)(2,1)S(1)}, bf16[4,1024]{1,0:T(4,128)(2,1)}, u32[]{:S(2)}) copy-start(bf16[4,1024]{1,0:T(4,128)(2,1)} %param.13) | copy-start | bytes 24580
  140.4 35.6 %copy-start.4 = (bf16[1024,512]{1,0:T(8,128)(2,1)S(1)}, bf16[1024,512]{1,0:T(8,128)(2,1)}, u32[]{:S(2)}) copy-start(bf16[1024,512]{1,0:T(8,128)(2,1)} %copy-done.3) | copy-start | bytes 3145732
  175.9 1.4 copy-start.6

commit v3 on v2

--- a/solution.py
+++ b/solution.py
@@ -26,20 +26,24 @@
     return dbag.astype(jnp.bfloat16)
 
 
-def owner_kernel(got_ref, table_ref, partial_ref, dense_ref):
-    groups, _, block_rows = got_ref.shape
-    per_p = partial_ref.shape[1]
-    blocks_dev = table_ref.shape[0] // block_rows
-    width = table_ref.shape[1]
-    got = got_ref[...].astype(jnp.float32)
-    row = got[:, per_p : per_p + 1, :]
-    shape = (groups, per_p, block_rows)
+def slot_blocks(got, per_p):
+    shape = (got.shape[0], per_p, got.shape[2])
     diagonal = lax.broadcasted_iota(jnp.int32, shape, 1) == lax.broadcasted_iota(
         jnp.int32, shape, 2
     )
-    block = jnp.sum(jnp.where(diagonal, row, 0.0), axis=2, keepdims=True)
+    row = got[:, per_p : per_p + 1, :]
+    return jnp.sum(jnp.where(diagonal, row, 0.0), axis=2, keepdims=True)
+
+
+def owner_kernel(got_ref, target_ref, table_ref, partial_ref, member_ref, dense_ref):
+    protein = lax.broadcasted_iota(jnp.int32, member_ref.shape, 0)
+    member_ref[...] = jnp.where(target_ref[...] == protein, 1.0, 0.0).astype(jnp.bfloat16)
+    groups, per_p, width = partial_ref.shape
+    block_rows = got_ref.shape[2]
+    got = got_ref[...].astype(jnp.float32)
+    block = slot_blocks(got, per_p)
     weights = got[:, :per_p, :]
-    for b in range(blocks_dev):
+    for b in range(table_ref.shape[0] // block_rows):
         mine = jnp.where(block == b, weights, 0.0).astype(jnp.bfloat16)
         dense_ref[:, b * block_rows : (b + 1) * block_rows] = mine.reshape(
             groups * per_p, block_rows
@@ -51,7 +55,56 @@
     )
 
 
-def owner_partials(got, table, per_p):
+def update_kernel(got_ref, grad_ref, table_ref, accum_ref, table_out, accum_out):
+    groups, per_p, width = grad_ref.shape
+    block_rows = got_ref.shape[2]
+    got = got_ref[...].astype(jnp.float32)
+    mine = jnp.where(slot_blocks(got, per_p) == pl.program_id(0), got[:, :per_p, :], 0.0)
+    grad = lax.dot_general(
+        mine.astype(jnp.bfloat16).reshape(groups * per_p, block_rows),
+        grad_ref[...].reshape(groups * per_p, width),
+        (((0,), (0,)), ((), ())),
+        preferred_element_type=jnp.float32,
+    )
+    square = (block_rows, block_rows)
+    diagonal = lax.broadcasted_iota(jnp.int32, square, 0) == lax.broadcasted_iota(
+        jnp.int32, square, 1
+    )
+    accum = jnp.sum(jnp.where(diagonal, accum_ref[0], 0.0), axis=1, keepdims=True)
+    accum = accum + jnp.mean(grad * grad, axis=1, keepdims=True)
+    rate = 0.3 / (jnp.sqrt(accum) + 1e-08)
+    table_out[...] = (table_ref[...].astype(jnp.float32) - grad * rate).astype(jnp.bfloat16)
+    accum_out[0] = jnp.sum(jnp.where(diagonal, accum, 0.0), axis=0, keepdims=True)
+
+
+def update_rows(got, grad, table, accum):
+    npl, rows, block_rows = got.shape
+    _, per_p, width = grad.shape
+    blocks = table.shape[0] // block_rows
+    whole = lambda i: (0, 0, 0)
+    table_spec = pl.BlockSpec((block_rows, width), lambda i: (i, 0))
+    accum_spec = pl.BlockSpec((1, 1, block_rows), lambda i: (i, 0, 0))
+    new_table, new_accum = pl.pallas_call(
+        update_kernel,
+        grid=(blocks,),
+        in_specs=[
+            pl.BlockSpec(got.shape, whole),
+            pl.BlockSpec(grad.shape, whole),
+            table_spec,
+            accum_spec,
+        ],
+        out_specs=[table_spec, accum_spec],
+        out_shape=[
+            jax.ShapeDtypeStruct(table.shape, table.dtype),
+            jax.ShapeDtypeStruct((blocks, 1, block_rows), jnp.float32),
+        ],
+        compiler_params=pltpu.CompilerParams(vmem_limit_bytes=24 * 2**20),
+        name="update_rows",
+    )(got, grad, table, accum.reshape(blocks, 1, block_rows))
+    return new_table, new_accum.reshape(accum.shape)
+
+
+def owner_partials(got, target, table, per_p, sums):
     npl, rows, block_rows = got.shape
     rows_dev, width = table.shape
     step = 8
@@ -60,19 +113,49 @@
         grid=(npl // step,),
         in_specs=[
             pl.BlockSpec((step, rows, block_rows), lambda i: (i, 0, 0)),
+            pl.BlockSpec((1, step * per_p), lambda i: (0, i)),
             pl.BlockSpec((rows_dev, width), lambda i: (0, 0)),
         ],
         out_specs=[
             pl.BlockSpec((step, per_p, width), lambda i: (i, 0, 0)),
-            pl.BlockSpec((step * per_p, rows_dev), lambda i: (i, 0)),
+            pl.BlockSpec((sums, step * per_p), lambda i: (0, i)),
         ],
         out_shape=[
             jax.ShapeDtypeStruct((npl, per_p, width), jnp.bfloat16),
-            jax.ShapeDtypeStruct((npl * per_p, rows_dev), jnp.bfloat16),
-        ],
+            jax.ShapeDtypeStruct((sums, npl * per_p), jnp.bfloat16),
+        ],
+        scratch_shapes=[pltpu.VMEM((step * per_p, rows_dev), jnp.bfloat16)],
         compiler_params=pltpu.CompilerParams(vmem_limit_bytes=24 * 2**20),
         name="owner_partials",
-    )(got, table)
+    )(got, target, table)
+
+
+def sum_kernel(member_ref, got_ref, out_ref):
+    slots = got_ref.shape[0] * got_ref.shape[1]
+    total = jnp.dot(
+        member_ref[...],
+        got_ref[...].reshape(slots, got_ref.shape[2]),
+        preferred_element_type=jnp.float32,
+    )
+    out_ref[...] = total.reshape(out_ref.shape)
+
+
+def protein_sums(member, got, nz):
+    sums, slots = member.shape
+    npl, per_p, width = got.shape
+    step = 256
+    return pl.pallas_call(
+        sum_kernel,
+        grid=(width // step,),
+        in_specs=[
+            pl.BlockSpec((sums, slots), lambda i: (0, 0)),
+            pl.BlockSpec((npl, per_p, step), lambda i: (0, 0, i)),
+        ],
+        out_specs=pl.BlockSpec((nz, sums // nz, step), lambda i: (0, 0, i)),
+        out_shape=jax.ShapeDtypeStruct((nz, sums // nz, width), jnp.float32),
+        compiler_params=pltpu.CompilerParams(vmem_limit_bytes=16 * 2**20),
+        name="protein_sums",
+    )(member, got)
 
 
 def exchange(x, axes):
@@ -130,17 +213,15 @@
     got2 = exchange(
         jnp.concatenate([w1.reshape(npl, per_p, block_rows), blk_rows], axis=1), PLANE
     )
-    partial_value, dense = owner_partials(got2, table, per_p)
-
-    got3 = exchange(partial_value, PLANE).reshape(slots, width)
     prot1 = lax.shift_right_arithmetic(code1, blocks_dev.bit_length() - 1)
     zs = jnp.arange(nz, dtype=jnp.int32)
     target = prot1 + jnp.where(prot1 >= 0, zs[None, :, None] * proteins, 0)
-    member = (
-        target.reshape(1, slots) == jnp.arange(nz * proteins, dtype=jnp.int32)[:, None]
-    ).astype(jnp.bfloat16)
-    bag_part = jnp.dot(member, got3, preferred_element_type=jnp.float32)
-    bag = jnp.sum(exchange(bag_part.reshape(nz, proteins, width), "z"), axis=0)
+    partial_value, member = owner_partials(
+        got2, target.reshape(1, slots), table, per_p, nz * proteins
+    )
+
+    bag_part = protein_sums(member, exchange(partial_value, PLANE), nz)
+    bag = jnp.sum(exchange(bag_part, "z"), axis=0)
 
     dbag = mlp_grad(bag, w_hidden, hidden_cot)
 
@@ -149,13 +230,8 @@
     send_g = lax.dot_general(
         member, every, (((0,), (0,)), ((), ())), preferred_element_type=jnp.float32
     ).astype(jnp.bfloat16)
-    got_grad = exchange(send_g.reshape(npl, per_p, width), PLANE).reshape(slots, width)
-    grad = lax.dot_general(
-        dense, got_grad, (((0,), (0,)), ((), ())), preferred_element_type=jnp.float32
-    )
-    acc_new = accum + jnp.mean(grad * grad, axis=-1)
-    rows_new = table.astype(jnp.float32) - 0.3 * grad / (jnp.sqrt(acc_new)[:, None] + 1e-08)
-    return (rows_new.astype(jnp.bfloat16), acc_new)
+    got_grad = exchange(send_g.reshape(npl, per_p, width), PLANE)
+    return update_rows(got2, got_grad, table, accum)
 
 
 def solution(mesh):

time: 180 us -> 180 us (level)
  waiting for transfers between devices: 27.9 us -> 7.25 us
  blocking collectives: 129 us -> 138 us
  starting transfers between devices: 4.71 us -> 13.6 us
  Pallas kernels: 2.04 us -> 7.65 us
  matrix products: 6.66 us -> 4.12 us
    all_to_all x1, waiting for transfers between devices: 27.9 us -> 7.25 us  [exchange(): return lax.all_to_all(x, axes, split_axis=0, concat_axis=0, tiled=True)]
    all_to_all x1, starting transfers between devices: 4.71 us -> 13.6 us  [exchange(): return lax.all_to_all(x, axes, split_axis=0, concat_axis=0, tiled=True)]
    all_to_all x5, blocking collectives: 129 us -> 138 us  [exchange(): return lax.all_to_all(x, axes, split_axis=0, concat_axis=0, tiled=True)]
    pallas_call x0 -> x2, Pallas kernels: none -> 5.59 us  [the longest x1 4.39 us: update_rows(): pl.pallas_call(update_kernel, grid=(blocks,), in_specs=[pl.BlockSpec(got....]
    dot_general x2 -> x0, matrix products: 3.46 us -> none  [the longest x1 2.11 us: per_device(): bag_part = jnp.dot(member, got3, preferred_element_type=jnp.float32)]
    unnamed x15 -> x11, local copies, waits for them, and re-layouts: 2.46 us -> 0.21 us
  transfers between devices with their start and end apart: 1 -> 1, of which waited for: 1 -> 1; matrix products, arithmetic and copies ran while one was open for 0% -> 1% of each run, Pallas kernels for 0% -> 0%
where the time goes in v3:
time: 180 us
  blocking collectives  138 us (77%)
  starting transfers between devices  13.6 us (8%)
  Pallas kernels  7.65 us (4%)
  waiting for transfers between devices  7.25 us (4%)
  local copies, waits for them, and re-layouts  4.59 us (3%)
  matrix products  4.12 us (2%)
  other arithmetic  3.53 us (2%)
    all_to_all x5, blocking collectives, exchange(): return lax.all_to_all(x, axes, split_axis=0, concat_axis=0, tiled=True)  138 us
    all_to_all x1, starting transfers between devices, exchange(): return lax.all_to_all(x, axes, split_axis=0, concat_axis=0, tiled=True)  13.6 us
    all_to_all x1, waiting for transfers between devices, exchange(): return lax.all_to_all(x, axes, split_axis=0, concat_axis=0, tiled=True)  7.25 us
    pallas_call x1, Pallas kernels, update_rows(): pl.pallas_call(update_kernel, grid=(blocks,), in_specs=[pl.BlockSpec(got....  4.39 us
  transfers between devices with their start and end apart: 1, of which 1 were waited for; matrix products, arithmetic and copies ran while one was open for 1% of the time, Pallas kernels for 0%

profile of v3, /device:TPU:1, one launch (start us, length us, event | category | flops | bytes accessed | tf_op | source)
XLA Modules:
  0.0 179.8 jit_solution(13962120889925217451)
XLA Ops:
  0.6 0.0 copy-start
  0.7 0.9 add_select_fusion.5
  1.5 0.2 convert_reduce_fusion
  1.8 0.4 select_reduce_fusion
  2.2 0.1 convert_element_type.67
  2.2 1.4 fusion.1
  3.7 29.4 %all_to_all.30 = bf16[16,72,128]{2,1,0:T(8,128)(2,1)S(1)} all-to-all(bf16[16,72,128]{2,1,0:T(8,128)(2,1)S(1)} %fusion.7), channel_id=1, replica_groups=mesh['xl'=2,'y'=4,'c'=2,'z'=16,'xh'=2] {'z'}, dimensions={0} | all-to-all | bytes 589824 | tf_op jit(solution)/shard_map/all_to_all | solution.py:162
  33.1 0.2 copy.41
  33.3 0.2 copy.34
  33.6 0.1 copy.36
  33.7 0.1 copy.37
  33.7 0.1 copy.38
  33.8 0.8 fusion.6
  34.6 13.6 %all-to-all-start.1 = ((bf16[32,40,128]{2,1,0:T(8,128)(2,1)}), bf16[32,40,128]{2,1,0:T(8,128)(2,1)S(1)}, u32[]{:S(2)}, u32[]{:S(2)}) async-start(bf16[32,40,128]{2,1,0:T(8,128)(2,1)} %fusion.6), calls=%async_computation.1 | async-start | bytes 655360 | tf_op jit(solution)/shard_map/all_to_all | solution.py:162
  48.2 0.1 copy.39
  48.3 1.0 copy.40
  49.2 1.1 reshape.81.target_ref
  50.4 7.2 %all-to-all-done.1.got_ref = bf16[32,40,128]{2,1,0:T(8,128)(2,1)S(1)} async-done(((bf16[32,40,128]{2,1,0:T(8,128)(2,1)}), bf16[32,40,128]{2,1,0:T(8,128)(2,1)S(1)}, u32[]{:S(2)}, u32[]{:S(2)}) %all-to-all-start.1) | async-done | bytes 327712 | tf_op jit(solution)/shard_map/all_to_all | solution.py:162
  57.6 2.1 %owner_partials.1 = (bf16[32,32,1024]{2,1,0:T(8,128)(2,1)S(1)}, bf16[64,1024]{1,0:T(8,128)(2,1)S(1)}) custom-call(bf16[32,40,128]{2,1,0:T(8,128)(2,1)S(1)} %all-to-all-done.1.got_ref, s32[1,1024]{1,0:T(1,128)S(1)} %reshape.81.target_ref, bf16[512,1024]{1,0:T(8,128)(2,1)S(1)} %copy-done.1), custom_call_target="tpu_custom_call" | custom-call | tf_op jit(solution)/shard_map/owner_partials/pallas_call | solution.py:111
  59.7 0.0 copy-start.2
  59.7 31.7 %all_to_all.31.got_ref = bf16[32,32,1024]{2,1,0:T(8,128)(2,1)S(1)} all-to-all(bf16[32,32,1024]{2,1,0:T(8,128)(2,1)S(1)} %get-tuple-element.7), channel_id=1, replica_groups=mesh['xl'=2,'y'=4,'c'=2,'z'=16,'xh'=2] {'xl','y','c','xh'}, dimensions={0} | all-to-all | bytes 4194304 | tf_op jit(solution)/shard_map/all_to_all | solution.py:162
  91.4 1.2 protein_sums.1
  92.6 18.9 %all_to_all.32 = f32[16,4,1024]{2,1,0:T(4,128)} all-to-all(f32[16,4,1024]{2,1,0:T(4,128)S(1)} %protein_sums.1), channel_id=1, replica_groups=mesh['xl'=2,'y'=4,'c'=2,'z'=16,'xh'=2] {'z'}, dimensions={0} | all-to-all | bytes 524288 | tf_op jit(solution)/shard_map/all_to_all | solution.py:162
  111.6 1.0 reduce_sum.37
  112.6 0.1 multiply_reduce_fusion.1
  112.7 1.1 multiply_reduce_fusion
  113.8 0.1 multiply_convert_fusion
  113.9 22.9 %all_to_all.33 = bf16[16,4,1024]{2,1,0:T(4,128)(2,1)} all-to-all(bf16[16,4,1024]{2,1,0:T(4,128)(2,1)S(1)} %broadcast_in_dim.27), channel_id=1, replica_groups=mesh['xl'=2,'y'=4,'c'=2,'z'=16,'xh'=2] {'z'}, dimensions={0} | all-to-all | bytes 262144 | tf_op jit(solution)/shard_map/all_to_all | solution.py:162
  136.9 1.6 reshape.82
  138.5 1.7 convolution_convert_fusion
  140.2 35.2 %all_to_all.34.grad_ref = bf16[32,32,1024]{2,1,0:T(8,128)(2,1)S(1)} all-to-all(bf16[32,32,1024]{2,1,0:T(8,128)(2,1)S(1)} %bitcast.21), channel_id=1, replica_groups=mesh['xl'=2,'y'=4,'c'=2,'z'=16,'xh'=2] {'xl','y','c','xh'}, dimensions={0} | all-to-all | bytes 4194304 | tf_op jit(solution)/shard_map/all_to_all | solution.py:162
  175.4 4.4 %update_rows.1 = (bf16[512,1024]{1,0:T(8,128)(2,1)}, f32[4,1,128]{2,1,0:T(1,128)}) custom-call(bf16[32,40,128]{2,1,0:T(8,128)(2,1)S(1)} %all-to-all-done.1.got_ref, bf16[32,32,1024]{2,1,0:T(8,128)(2,1)S(1)} %all_to_all.34.grad_ref, bf16[512,1024]{1,0:T(8,128)(2,1)S(1)} %copy-done.1, f32[4,1,128]{2,1,0:T(1,128)S(1)} %bitcast.20), custom_call_target="tpu_custom_call" | custom-call | tf_op jit(solution)/shard_map/update_rows/pallas_call | solution.py:87
  (19 shorter events, 0.2 us)
Async XLA Ops:
  0.6 112.1 %copy-start = (bf16[1024,1024]{1,0:T(8,128)(2,1)S(1)}, bf16[1024,1024]{1,0:T(8,128)(2,1)}, u32[]{:S(2)}) copy-start(bf16[1024,1024]{1,0:T(8,128)(2,1)} %param.12) | copy-start | bytes 6291460
  3.7 54.0 %copy-start.1 = (bf16[512,1024]{1,0:T(8,128)(2,1)S(1)}, bf16[512,1024]{1,0:T(8,128)(2,1)}, u32[]{:S(2)}) copy-start(bf16[512,1024]{1,0:T(8,128)(2,1)} %table_ref.3) | copy-start | bytes 3145732
  34.6 23.0 %all-to-all-start.1 = ((bf16[32,40,128]{2,1,0:T(8,128)(2,1)}), bf16[32,40,128]{2,1,0:T(8,128)(2,1)S(1)}, u32[]{:S(2)}, u32[]{:S(2)}) async-start(bf16[32,40,128]{2,1,0:T(8,128)(2,1)} %fusion.6), calls=%async_computation.1 | async-start | bytes 655360 | tf_op jit(solution)/shard_map/all_to_all | solution.py:162
  59.7 31.7 %copy-start.2 = (bf16[64,1024]{1,0:T(8,128)(2,1)}, bf16[64,1024]{1,0:T(8,128)(2,1)S(1)}, u32[]{:S(2)}) copy-start(bf16[64,1024]{1,0:T(8,128)(2,1)S(1)} %get-tuple-element.6.member_ref) | copy-start | bytes 393220
  91.4 21.3 %copy-start.4 = (bf16[4,1024]{1,0:T(4,128)(2,1)S(1)}, bf16[4,1024]{1,0:T(4,128)(2,1)}, u32[]{:S(2)}) copy-start(bf16[4,1024]{1,0:T(4,128)(2,1)} %param.13) | copy-start | bytes 24580
  140.2 35.2 %copy-start.3 = (f32[512]{0:T(512)S(1)}, f32[512]{0:T(512)}, u32[]{:S(2)}) copy-start(f32[512]{0:T(512)} %param.8) | copy-start | bytes 6148

commit v4 on v3

v4 whole, which is shorter than its diff:
```python
import functools

import jax
import jax.numpy as jnp
from jax import lax
from jax.experimental import pallas as pl
from jax.experimental.pallas import tpu as pltpu
from jax.sharding import Mesh
from jax.sharding import PartitionSpec as P

CAP = 2
BLK_DEV = 4
AXES = ("xl", "y", "c", "z", "xh")
SIZES = (2, 4, 2, 16, 2)
PLANE = ("xl", "y", "c", "xh")


def dense_layer_kernel(sums_ref, w_ref, cot_ref, out_ref):
    nz = sums_ref.shape[0]
    bag = sums_ref[0]
    for z in range(1, nz):
        bag = bag + sums_ref[z]
    inv = lax.rsqrt(jnp.mean(bag * bag, axis=-1, keepdims=True) + 1e-06)
    unit = bag * inv
    pre = jnp.dot(unit.astype(jnp.bfloat16), w_ref[...], preferred_element_type=jnp.float32)
    sig = jax.nn.sigmoid(pre)
    dpre = (cot_ref[...].astype(jnp.float32) * sig * (1.0 + pre * (1.0 - sig))).astype(
        jnp.bfloat16
    )
    dunit = lax.dot_general(
        dpre, w_ref[...], (((1,), (1,)), ((), ())), preferred_element_type=jnp.float32
    )
    dbag = (dunit - unit * jnp.mean(dunit * unit, axis=-1, keepdims=True)) * inv
    out_ref[...] = jnp.broadcast_to(dbag.astype(jnp.bfloat16)[None], out_ref.shape)


def dense_layer(sums, w_hidden, hidden_cot):
    return pl.pallas_call(
        dense_layer_kernel,
        out_shape=jax.ShapeDtypeStruct(sums.shape, jnp.bfloat16),
        compiler_params=pltpu.CompilerParams(vmem_limit_bytes=16 * 2**20),
        name="dense_layer",
    )(sums, w_hidden, hidden_cot)


def route_kernel(nh, proteins, block_ref, protein_ref, weight_ref, out_ref):
    nz, rows, block_rows = out_ref.shape
    pairs = block_ref.shape[1]
    per_z = rows - 8
    slots = nz * per_z
    block = block_ref[...]
    owner = block // BLK_DEV
    code = (protein_ref[...] % proteins) * BLK_DEV + block % BLK_DEV + 1

    square = (pairs, pairs)
    down = lax.broadcasted_iota(jnp.int32, square, 0)
    across = lax.broadcasted_iota(jnp.int32, square, 1)
    owner_f = owner.astype(jnp.float32)
    column = jnp.sum(jnp.where(down == across, owner_f, 0.0), axis=1, keepdims=True)
    earlier = jnp.where((column == owner_f) & (down < across), 1.0, 0.0)
    rank = jnp.sum(earlier, axis=0, keepdims=True).astype(jnp.int32)

    oz = (owner % (nz * nh)) // nh
    opl = (owner // (nz * nh)) * nh + owner % nh
    within = opl * CAP + rank
    slot = oz * per_z + within
    place = lax.broadcasted_iota(jnp.int32, (slots, pairs), 0) == slot
    send = jnp.dot(
        jnp.where(place, 1.0, 0.0).astype(jnp.bfloat16),
        weight_ref[...],
        preferred_element_type=jnp.float32,
    )
    mine = lax.broadcasted_iota(jnp.int32, (nz, pairs), 0) == oz
    lane = lax.broadcasted_iota(jnp.int32, (block_rows, pairs), 0) == within
    codes = lax.dot_general(
        jnp.where(mine, code.astype(jnp.float32), 0.0).astype(jnp.bfloat16),
        jnp.where(lane, 1.0, 0.0).astype(jnp.bfloat16),
        (((1,), (1,)), ((), ())),
        preferred_element_type=jnp.float32,
    )
    out_ref[...] = jnp.concatenate(
        [
            send.reshape(nz, per_z, block_rows),
            jnp.broadcast_to(codes[:, None, :], (nz, 8, block_rows)),
        ],
        axis=1,
    ).astype(jnp.bfloat16)


def route(pair_block, pair_protein, pair_weight, nz, nh, per_z, proteins):
    pairs, block_rows = pair_weight.shape
    return pl.pallas_call(
        functools.partial(route_kernel, nh, proteins),
        out_shape=jax.ShapeDtypeStruct((nz, per_z + 8, block_rows), jnp.bfloat16),
        compiler_params=pltpu.CompilerParams(vmem_limit_bytes=16 * 2**20),
        name="route",
    )(
        pltpu.with_memory_space_constraint(pair_block.reshape(1, pairs), pltpu.HBM),
        pltpu.with_memory_space_constraint(pair_protein.reshape(1, pairs), pltpu.HBM),
        pltpu.with_memory_space_constraint(pair_weight, pltpu.HBM),
    )


def slot_blocks(got, per_p):
    shape = (got.shape[0], per_p, got.shape[2])
    diagonal = lax.broadcasted_iota(jnp.int32, shape, 1) == lax.broadcasted_iota(
        jnp.int32, shape, 2
    )
    row = got[:, per_p : per_p + 1, :]
    return jnp.sum(jnp.where(diagonal, row, 0.0), axis=2, keepdims=True)


def fill_dense(got, per_p, dense_ref):
    groups, _, block_rows = got.shape
    block = slot_blocks(got, per_p)
    weights = got[:, :per_p, :]
    for b in range(dense_ref.shape[1] // block_rows):
        mine = jnp.where(block == b, weights, 0.0).astype(jnp.bfloat16)
        dense_ref[:, b * block_rows : (b + 1) * block_rows] = mine.reshape(
            groups * per_p, block_rows
        )


def owner_kernel(got_ref, table_ref, partial_ref, dense_ref):
    fill_dense(got_ref[...].astype(jnp.float32), partial_ref.shape[1], dense_ref)
    partial_ref[...] = (
        jnp.dot(dense_ref[...], table_ref[...], preferred_element_type=jnp.float32)
        .astype(jnp.bfloat16)
        .reshape(partial_ref.shape)
    )


def update_kernel(
    got_ref,
    grad_ref,
    accum_ref,
    table_ref,
    table_out,
    accum_out,
    dense_ref,
    sum_ref,
    new_ref,
    out_sems,
):
    groups, per_p, width = grad_ref.shape
    block_rows = got_ref.shape[2]
    blocks = table_ref.shape[0] // block_rows
    fill_dense(got_ref[...].astype(jnp.float32), per_p, dense_ref)
    sum_ref[...] = lax.dot_general(
        dense_ref[...],
        grad_ref[...].reshape(groups * per_p, width),
        (((0,), (0,)), ((), ())),
        preferred_element_type=jnp.float32,
    )
    square = (block_rows, block_rows)
    diagonal = lax.broadcasted_iota(jnp.int32, square, 0) == lax.broadcasted_iota(
        jnp.int32, square, 1
    )
    stores = []
    for b in range(blocks):
        rows = pl.ds(b * block_rows, block_rows)
        grad = sum_ref[rows, :]
        accum = jnp.sum(jnp.where(diagonal, accum_ref[b], 0.0), axis=1, keepdims=True)
        accum = accum + jnp.mean(grad * grad, axis=1, keepdims=True)
        rate = 0.3 / (jnp.sqrt(accum) + 1e-08)
        new_ref[rows, :] = (table_ref[rows, :].astype(jnp.float32) - grad * rate).astype(
            jnp.bfloat16
        )
        accum_out[b] = jnp.sum(jnp.where(diagonal, accum, 0.0), axis=0, keepdims=True)
        store = pltpu.make_async_copy(new_ref.at[rows, :], table_out.at[rows, :], out_sems.at[b])
        store.start()
        stores.append(store)
    for store in stores:
        store.wait()


def update_rows(got, grad, table, accum):
    npl, rows, block_rows = got.shape
    _, per_p, width = grad.shape
    rows_dev = table.shape[0]
    blocks = rows_dev // block_rows
    vmem = pl.BlockSpec(memory_space=pltpu.VMEM)
    anywhere = pl.BlockSpec(memory_space=pl.ANY)
    new_table, new_accum = pl.pallas_call(
        update_kernel,
        in_specs=[vmem, vmem, vmem, vmem],
        out_specs=[anywhere, vmem],
        out_shape=[
            jax.ShapeDtypeStruct(table.shape, table.dtype),
            jax.ShapeDtypeStruct((blocks, 1, block_rows), jnp.float32),
        ],
        scratch_shapes=[
            pltpu.VMEM((npl * per_p, rows_dev), jnp.bfloat16),
            pltpu.VMEM((rows_dev, width), jnp.float32),
            pltpu.VMEM((rows_dev, width), table.dtype),
            pltpu.SemaphoreType.DMA((blocks,)),
        ],
        compiler_params=pltpu.CompilerParams(vmem_limit_bytes=24 * 2**20),
        name="update_rows",
    )(got, grad, accum.reshape(blocks, 1, block_rows), table)
    return new_table, new_accum.reshape(accum.shape)


def owner_partials(got, table, per_p):
    npl, rows, block_rows = got.shape
    rows_dev, width = table.shape
    return pl.pallas_call(
        owner_kernel,
        out_shape=jax.ShapeDtypeStruct((npl, per_p, width), jnp.bfloat16),
        scratch_shapes=[pltpu.VMEM((npl * per_p, rows_dev), jnp.bfloat16)],
        compiler_params=pltpu.CompilerParams(vmem_limit_bytes=24 * 2**20),
        name="owner_partials",
    )(got, table)


def membership(codes, proteins, per_p, slots):
    nz, lanes = codes.shape
    sums = nz * proteins
    source = lax.broadcasted_iota(jnp.int32, (sums, nz), 0) // proteins
    spread = source == lax.broadcasted_iota(jnp.int32, (sums, nz), 1)
    by_row = jnp.dot(
        jnp.where(spread, 1.0, 0.0).astype(jnp.bfloat16),
        codes,
        preferred_element_type=jnp.float32,
    ).astype(jnp.bfloat16)
    slot = lax.broadcasted_iota(jnp.int32, (lanes, slots), 1)
    entry = (slot // per_p) * CAP + slot % CAP
    move = lax.broadcasted_iota(jnp.int32, (lanes, slots), 0) == entry
    code = jnp.dot(
        by_row, jnp.where(move, 1.0, 0.0).astype(jnp.bfloat16), preferred_element_type=jnp.float32
    ).astype(jnp.int32)
    row = lax.broadcasted_iota(jnp.int32, (sums, slots), 0)
    slot = lax.broadcasted_iota(jnp.int32, (sums, slots), 1)
    low = (row % proteins) * BLK_DEV
    mine = (row // proteins == (slot % per_p) // CAP) & (code > low) & (code <= low + BLK_DEV)
    return jnp.where(mine, 1.0, 0.0).astype(jnp.bfloat16)


def sum_kernel(codes_ref, got_ref, out_ref, member_ref):
    proteins = out_ref.shape[1]
    _, per_p, width = got_ref.shape
    slots = member_ref.shape[1]
    member_ref[...] = membership(codes_ref[...], proteins, per_p, slots)
    total = jnp.dot(
        member_ref[...], got_ref[...].reshape(slots, width), preferred_element_type=jnp.float32
    )
    out_ref[...] = total.reshape(out_ref.shape)


def protein_sums(codes, got, proteins):
    nz = codes.shape[0]
    npl, per_p, width = got.shape
    return pl.pallas_call(
        sum_kernel,
        out_shape=[
            jax.ShapeDtypeStruct((nz, proteins, width), jnp.float32),
            jax.ShapeDtypeStruct((nz * proteins, npl * per_p), jnp.bfloat16),
        ],
        compiler_params=pltpu.CompilerParams(vmem_limit_bytes=16 * 2**20),
        name="protein_sums",
    )(codes, got)


def select_kernel(member_ref, every_ref, out_ref):
    nz, proteins, width = every_ref.shape
    picked = lax.dot_general(
        member_ref[...],
        every_ref[...].astype(jnp.float32).reshape(nz * proteins, width).astype(jnp.bfloat16),
        (((0,), (0,)), ((), ())),
        preferred_element_type=jnp.float32,
    )
    out_ref[...] = picked.astype(jnp.bfloat16).reshape(out_ref.shape)


def select_grads(member, every, npl):
    slots = member.shape[1]
    width = every.shape[2]
    return pl.pallas_call(
        select_kernel,
        out_shape=jax.ShapeDtypeStruct((npl, slots // npl, width), jnp.bfloat16),
        compiler_params=pltpu.CompilerParams(vmem_limit_bytes=16 * 2**20),
        name="select_grads",
    )(member, every)


def exchange(x, axes):
    return lax.all_to_all(x, axes, split_axis=0, concat_axis=0, tiled=True)


def per_device(table, accum, pair_block, pair_protein, pair_weight, w_hidden, hidden_cot):
    nz = lax.axis_size("z")
    npl = lax.axis_size(PLANE)
    block_rows = pair_weight.shape[1]
    proteins, width = hidden_cot.shape
    per_z = npl * CAP
    per_p = nz * CAP

    first = route(
        pair_block, pair_protein, pair_weight, nz, lax.axis_size("xh"), per_z, proteins
    )
    first = exchange(first, "z")

    weights = first[:, :per_z].reshape(nz, npl, CAP, block_rows).transpose(1, 0, 2, 3)
    codes = lax.optimization_barrier(first[:, per_z, :per_z])
    code = codes.astype(jnp.int32).reshape(nz, npl, CAP).transpose(1, 0, 2)
    block = ((code - 1) & (BLK_DEV - 1)).astype(jnp.bfloat16).reshape(npl, 1, per_p)
    block = jnp.pad(block, ((0, 0), (0, 7), (0, block_rows - per_p)))
    second = exchange(
        jnp.concatenate([weights.reshape(npl, per_p, block_rows), block], axis=1), PLANE
    )
    partial_value = owner_partials(second, table, per_p)

    sums, member = protein_sums(codes, exchange(partial_value, PLANE), proteins)
    dbag = dense_layer(exchange(sums, "z"), w_hidden, hidden_cot)

    every = exchange(dbag, "z")
    grad = exchange(select_grads(member, every, npl), PLANE)
    return update_rows(second, grad, table, accum)


def solution(mesh):
    split = Mesh(mesh.devices.reshape(SIZES), AXES)
    in_specs = (
        P(AXES, None),
        P(AXES),
        P(AXES),
        P(AXES),
        P(AXES, None),
        P(),
        P(AXES, None),
    )
    out_specs = (P(AXES, None), P(AXES))
    return jax.shard_map(
        per_device, mesh=split, in_specs=in_specs, out_specs=out_specs, check_vma=False
    )
```

time: 180 us -> 171 us (0.950)
  blocking collectives: 138 us -> 161 us
  starting transfers between devices: 13.6 us -> 0 us
  waiting for transfers between devices: 7.25 us -> 0 us
  matrix products: 4.12 us -> 0 us
  local copies, waits for them, and re-layouts: 4.59 us -> 0.51 us
  other arithmetic: 3.53 us -> 0.04 us
    all_to_all x5 -> x6, blocking collectives: 138 us -> 161 us  [exchange(): return lax.all_to_all(x, axes, split_axis=0, concat_axis=0, tiled=True)]
    all_to_all x1 -> x0, starting transfers between devices: 13.6 us -> none  [exchange(): return lax.all_to_all(x, axes, split_axis=0, concat_axis=0, tiled=True)]
    all_to_all x1 -> x0, waiting for transfers between devices: 7.25 us -> none  [exchange(): return lax.all_to_all(x, axes, split_axis=0, concat_axis=0, tiled=True)]
    dot_general x3 -> x0, matrix products: 4.12 us -> none  [the longest x1 1.69 us: per_device(): lax.dot_general(member, every, (((0,), (0,)), ((), ())), preferred_elemen...]
    reshape x3 -> x2, local copies, waits for them, and re-layouts: 2.81 us -> 0.28 us  [the longest x1 0.18 us: per_device(): first[:, :per_z].reshape(nz, npl, CAP, block_rows).transpose(1, 0, 2, 3)]
    pallas_call x3 -> x6, Pallas kernels: 7.65 us -> 9.03 us  [the longest x1 3.47 us: update_rows(): pl.pallas_call(update_kernel, in_specs=[vmem, vmem, vmem, vmem], out_spec...]
  transfers between devices with their start and end apart: 1 -> 0, of which waited for: 1 -> 0; matrix products, arithmetic and copies ran while one was open for 1% -> 0% of each run, Pallas kernels for 0% -> 0%
where the time goes in v4:
time: 171 us
  blocking collectives  161 us (94%)
  Pallas kernels  9.03 us (5%)
    all_to_all x6, blocking collectives, exchange(): return lax.all_to_all(x, axes, split_axis=0, concat_axis=0, tiled=True)  161 us
    pallas_call x1, Pallas kernels, update_rows(): pl.pallas_call(update_kernel, in_specs=[vmem, vmem, vmem, vmem], out_spec...  3.47 us

profile of v4, /device:TPU:1, one launch (start us, length us, event | category | flops | bytes accessed | tf_op | source)
XLA Modules:
  0.0 171.0 jit_solution(12155348758989656305)
XLA Ops:
  0.6 0.0 copy-start
  0.6 1.6 route.1
  2.3 29.3 %all_to_all.30 = bf16[16,72,128]{2,1,0:T(8,128)(2,1)S(1)} all-to-all(bf16[16,72,128]{2,1,0:T(8,128)(2,1)S(1)} %route.1), channel_id=1, replica_groups=mesh['xl'=2,'y'=4,'c'=2,'z'=16,'xh'=2] {'z'}, dimensions={0} | all-to-all | bytes 589824 | tf_op jit(solution)/shard_map/all_to_all | solution.py:287
  31.6 0.2 copy.17
  31.8 0.1 copy.19
  31.9 0.1 copy.20
  32.0 0.1 copy.21
  32.2 22.8 %all_to_all.31.got_ref = bf16[32,40,128]{2,1,0:T(8,128)(2,1)S(1)} all-to-all(bf16[32,40,128]{2,1,0:T(8,128)(2,1)S(1)} %fusion.1), channel_id=1, replica_groups=mesh['xl'=2,'y'=4,'c'=2,'z'=16,'xh'=2] {'xl','y','c','xh'}, dimensions={0} | all-to-all | bytes 655360 | tf_op jit(solution)/shard_map/all_to_all | solution.py:287
  55.0 0.0 copy-done
  55.0 1.3 owner_partials.1
  56.3 31.7 %all_to_all.32.got_ref = bf16[32,32,1024]{2,1,0:T(8,128)(2,1)S(1)} all-to-all(bf16[32,32,1024]{2,1,0:T(8,128)(2,1)S(1)} %owner_partials.1), channel_id=1, replica_groups=mesh['xl'=2,'y'=4,'c'=2,'z'=16,'xh'=2] {'xl','y','c','xh'}, dimensions={0} | all-to-all | bytes 4194304 | tf_op jit(solution)/shard_map/all_to_all | solution.py:287
  88.0 0.0 copy-start.1
  88.0 0.0 copy-start.2
  88.0 0.8 protein_sums.1
  88.8 18.8 %all_to_all.33.sums_ref = f32[16,4,1024]{2,1,0:T(4,128)S(1)} all-to-all(f32[16,4,1024]{2,1,0:T(4,128)S(1)} %get-tuple-element.7), channel_id=1, replica_groups=mesh['xl'=2,'y'=4,'c'=2,'z'=16,'xh'=2] {'z'}, dimensions={0} | all-to-all | bytes 524288 | tf_op jit(solution)/shard_map/all_to_all | solution.py:287
  107.6 0.0 copy-done.1
  107.6 0.0 copy-done.2
  107.6 1.1 dense_layer.1
  108.8 22.8 %all_to_all.34.every_ref = bf16[16,4,1024]{2,1,0:T(4,128)(2,1)S(1)} all-to-all(bf16[16,4,1024]{2,1,0:T(4,128)(2,1)S(1)} %dense_layer.1), channel_id=1, replica_groups=mesh['xl'=2,'y'=4,'c'=2,'z'=16,'xh'=2] {'z'}, dimensions={0} | all-to-all | bytes 262144 | tf_op jit(solution)/shard_map/all_to_all | solution.py:287
  131.6 0.7 select_grads.1
  132.3 0.0 copy-start.3
  132.3 35.2 %all_to_all.35.grad_ref = bf16[32,32,1024]{2,1,0:T(8,128)(2,1)S(1)} all-to-all(bf16[32,32,1024]{2,1,0:T(8,128)(2,1)S(1)} %select_grads.1), channel_id=1, replica_groups=mesh['xl'=2,'y'=4,'c'=2,'z'=16,'xh'=2] {'xl','y','c','xh'}, dimensions={0} | all-to-all | bytes 4194304 | tf_op jit(solution)/shard_map/all_to_all | solution.py:287
  167.5 0.0 copy-done.3
  167.5 3.5 %update_rows.1 = (bf16[512,1024]{1,0:T(8,128)(2,1)}, f32[4,1,128]{2,1,0:T(1,128)}) custom-call(bf16[32,40,128]{2,1,0:T(8,128)(2,1)S(1)} %all_to_all.31.got_ref, bf16[32,32,1024]{2,1,0:T(8,128)(2,1)S(1)} %all_to_all.35.grad_ref, f32[4,1,128]{2,1,0:T(1,128)S(1)} %bitcast.17, bf16[512,1024]{1,0:T(8,128)(2,1)S(1)} %copy-done), custom_call_target="tpu_custom_call" | custom-call | tf_op jit(solution)/shard_map/update_rows/pallas_call | solution.py:184
  (5 shorter events, 0.1 us)
Async XLA Ops:
  0.6 54.4 %copy-start = (bf16[512,1024]{1,0:T(8,128)(2,1)S(1)}, bf16[512,1024]{1,0:T(8,128)(2,1)}, u32[]{:S(2)}) copy-start(bf16[512,1024]{1,0:T(8,128)(2,1)} %table_ref.3) | copy-start | bytes 3145732
  88.0 19.6 %copy-start.1 = (bf16[1024,1024]{1,0:T(8,128)(2,1)S(1)}, bf16[1024,1024]{1,0:T(8,128)(2,1)}, u32[]{:S(2)}) copy-start(bf16[1024,1024]{1,0:T(8,128)(2,1)} %w_ref.1) | copy-start | bytes 6291460
  88.0 19.6 %copy-start.2 = (bf16[4,1024]{1,0:T(4,128)(2,1)S(1)}, bf16[4,1024]{1,0:T(4,128)(2,1)}, u32[]{:S(2)}) copy-start(bf16[4,1024]{1,0:T(4,128)(2,1)} %cot_ref.1) | copy-start | bytes 24580
  132.3 35.2 %copy-start.3 = (f32[512]{0:T(512)S(1)}, f32[512]{0:T(512)}, u32[]{:S(2)}) copy-start(f32[512]{0:T(512)} %param.8) | copy-start | bytes 6148

commit v5 on v4

v5 whole, which is shorter than its diff:
```python
import functools

import jax
import jax.numpy as jnp
from jax import lax
from jax.experimental import pallas as pl
from jax.experimental.pallas import tpu as pltpu
from jax.sharding import Mesh
from jax.sharding import PartitionSpec as P

CAP = 2
BLK_DEV = 4
AXES = ("xl", "y", "c", "z", "zl", "xh")
SIZES = (2, 4, 2, 8, 2, 2)
LINE = ("zl", "z")
PLANE = ("xl", "y", "c", "xh")
GROUP = ("xl", "y", "c", "xh", "zl")


def dense_layer_kernel(sums_ref, w_ref, cot_ref, out_ref):
    nz = sums_ref.shape[0]
    bag = sums_ref[0]
    for z in range(1, nz):
        bag = bag + sums_ref[z]
    inv = lax.rsqrt(jnp.mean(bag * bag, axis=-1, keepdims=True) + 1e-06)
    unit = bag * inv
    pre = jnp.dot(unit.astype(jnp.bfloat16), w_ref[...], preferred_element_type=jnp.float32)
    sig = jax.nn.sigmoid(pre)
    dpre = (cot_ref[...].astype(jnp.float32) * sig * (1.0 + pre * (1.0 - sig))).astype(
        jnp.bfloat16
    )
    dunit = lax.dot_general(
        dpre, w_ref[...], (((1,), (1,)), ((), ())), preferred_element_type=jnp.float32
    )
    dbag = (dunit - unit * jnp.mean(dunit * unit, axis=-1, keepdims=True)) * inv
    lanes = out_ref.shape[2]
    rows = [dbag[:, j : j + lanes] for j in range(0, dbag.shape[1], lanes)]
    message = jnp.concatenate(rows, axis=0).astype(jnp.bfloat16)
    out_ref[...] = jnp.broadcast_to(message[None], out_ref.shape)


def dense_layer(sums, w_hidden, hidden_cot):
    nz, proteins, width = sums.shape
    return pl.pallas_call(
        dense_layer_kernel,
        out_shape=jax.ShapeDtypeStruct((nz, proteins * width // 128, 128), jnp.bfloat16),
        compiler_params=pltpu.CompilerParams(vmem_limit_bytes=16 * 2**20),
        name="dense_layer",
    )(sums, w_hidden, hidden_cot)


def route_kernel(
    nl, nh, proteins, block_in, protein_in, weight_in, out_ref, block_ref, protein_ref, weight_ref, sems
):
    copies = [
        pltpu.make_async_copy(source, target, sems.at[i])
        for i, (source, target) in enumerate(
            [(block_in, block_ref), (protein_in, protein_ref), (weight_in, weight_ref)]
        )
    ]
    for copy in copies:
        copy.start()
    for copy in copies:
        copy.wait()
    line, rows, block_rows = out_ref.shape
    pairs = block_ref.shape[1]
    per_z = rows - 8
    slots = line * per_z
    block = block_ref[...]
    owner = block // BLK_DEV
    code = (protein_ref[...] % proteins) * BLK_DEV + block % BLK_DEV + 1

    square = (pairs, pairs)
    down = lax.broadcasted_iota(jnp.int32, square, 0)
    across = lax.broadcasted_iota(jnp.int32, square, 1)
    owner_f = owner.astype(jnp.float32)
    column = jnp.sum(jnp.where(down == across, owner_f, 0.0), axis=1, keepdims=True)
    earlier = jnp.where((column == owner_f) & (down < across), 1.0, 0.0)
    rank = jnp.sum(earlier, axis=0, keepdims=True).astype(jnp.int32)

    n_dp = line * nh
    nz = line // nl
    along = (owner % n_dp) // nh
    z, zl = along // nl, along % nl
    plane = (owner // n_dp) * nh + owner % nh
    place = lax.broadcasted_iota(jnp.int32, (slots, pairs), 0) == (
        (zl * nz + z) * per_z + plane * CAP + rank
    )
    send = jnp.dot(
        jnp.where(place, 1.0, 0.0).astype(jnp.bfloat16),
        weight_ref[...],
        preferred_element_type=jnp.float32,
    )

    def code_rows(row, count, lane):
        mine = lax.broadcasted_iota(jnp.int32, (count, pairs), 0) == row
        here = lax.broadcasted_iota(jnp.int32, (block_rows, pairs), 0) == lane
        return lax.dot_general(
            jnp.where(mine, code.astype(jnp.float32), 0.0).astype(jnp.bfloat16),
            jnp.where(here, 1.0, 0.0).astype(jnp.bfloat16),
            (((1,), (1,)), ((), ())),
            preferred_element_type=jnp.float32,
        )

    own = code_rows(zl * nz + z, line, plane * CAP + rank)
    both = code_rows(z, nz, (plane * nl + zl) * CAP + rank)
    both = jnp.concatenate([both] * nl, axis=0)
    row = lax.broadcasted_iota(jnp.int32, (line, 8, block_rows), 1)
    out_ref[...] = jnp.concatenate(
        [
            send.reshape(line, per_z, block_rows),
            jnp.where(row == 0, own[:, None, :], both[:, None, :]),
        ],
        axis=1,
    ).astype(jnp.bfloat16)


def route(pair_block, pair_protein, pair_weight, line, nl, nh, per_z, proteins):
    pairs, block_rows = pair_weight.shape
    return pl.pallas_call(
        functools.partial(route_kernel, nl, nh, proteins),
        in_specs=[pl.BlockSpec(memory_space=pl.ANY)] * 3,
        out_shape=jax.ShapeDtypeStruct((line, per_z + 8, block_rows), jnp.bfloat16),
        scratch_shapes=[
            pltpu.VMEM((1, pairs), jnp.int32),
            pltpu.VMEM((1, pairs), jnp.int32),
            pltpu.VMEM((pairs, block_rows), jnp.bfloat16),
            pltpu.SemaphoreType.DMA((3,)),
        ],
        compiler_params=pltpu.CompilerParams(vmem_limit_bytes=16 * 2**20),
        name="route",
    )(
        pltpu.with_memory_space_constraint(pair_block.reshape(1, pairs), pltpu.HBM),
        pltpu.with_memory_space_constraint(pair_protein.reshape(1, pairs), pltpu.HBM),
        pltpu.with_memory_space_constraint(pair_weight, pltpu.HBM),
    )


def slot_blocks(got, per_p):
    shape = (got.shape[0], per_p, got.shape[2])
    diagonal = lax.broadcasted_iota(jnp.int32, shape, 1) == lax.broadcasted_iota(
        jnp.int32, shape, 2
    )
    row = got[:, per_p : per_p + 1, :]
    return jnp.sum(jnp.where(diagonal, row, 0.0), axis=2, keepdims=True)


def fill_dense(got, per_p, dense_ref):
    groups, _, block_rows = got.shape
    block = slot_blocks(got, per_p)
    weights = got[:, :per_p, :]
    for b in range(dense_ref.shape[1] // block_rows):
        mine = jnp.where(block == b, weights, 0.0).astype(jnp.bfloat16)
        dense_ref[:, b * block_rows : (b + 1) * block_rows] = mine.reshape(
            groups * per_p, block_rows
        )


def owner_kernel(got_ref, table_ref, partial_ref, dense_ref):
    fill_dense(got_ref[...].astype(jnp.float32), got_ref.shape[1] - 8, dense_ref)
    partial_ref[...] = (
        jnp.dot(dense_ref[...], table_ref[...], preferred_element_type=jnp.float32)
        .astype(jnp.bfloat16)
        .reshape(partial_ref.shape)
    )


def update_kernel(
    got_ref,
    grad_ref,
    accum_ref,
    table_ref,
    table_out,
    accum_out,
    dense_ref,
    sum_ref,
):
    slots = grad_ref.shape[0] * grad_ref.shape[1]
    width = grad_ref.shape[2]
    block_rows = got_ref.shape[2]
    blocks = table_ref.shape[0] // block_rows
    fill_dense(got_ref[...].astype(jnp.float32), got_ref.shape[1] - 8, dense_ref)
    sum_ref[...] = lax.dot_general(
        dense_ref[...],
        grad_ref[...].reshape(slots, width),
        (((0,), (0,)), ((), ())),
        preferred_element_type=jnp.float32,
    )
    square = (block_rows, block_rows)
    diagonal = lax.broadcasted_iota(jnp.int32, square, 0) == lax.broadcasted_iota(
        jnp.int32, square, 1
    )
    for b in range(blocks):
        rows = slice(b * block_rows, (b + 1) * block_rows)
        grad = sum_ref[rows, :]
        accum = jnp.sum(jnp.where(diagonal, accum_ref[b], 0.0), axis=1, keepdims=True)
        accum = accum + jnp.mean(grad * grad, axis=1, keepdims=True)
        rate = 0.3 / (jnp.sqrt(accum) + 1e-08)
        table_out[rows, :] = (table_ref[rows, :].astype(jnp.float32) - grad * rate).astype(
            jnp.bfloat16
        )
        accum_out[b] = jnp.sum(jnp.where(diagonal, accum, 0.0), axis=0, keepdims=True)


def update_rows(got, grad, table, accum):
    block_rows = got.shape[2]
    slots, width = grad.shape[0] * grad.shape[1], grad.shape[2]
    rows_dev = table.shape[0]
    blocks = rows_dev // block_rows
    new_table, new_accum = pl.pallas_call(
        update_kernel,
        out_shape=[
            jax.ShapeDtypeStruct(table.shape, table.dtype),
            jax.ShapeDtypeStruct((blocks, 1, block_rows), jnp.float32),
        ],
        scratch_shapes=[
            pltpu.VMEM((slots, rows_dev), jnp.bfloat16),
            pltpu.VMEM((rows_dev, width), jnp.float32),
        ],
        compiler_params=pltpu.CompilerParams(vmem_limit_bytes=24 * 2**20),
        name="update_rows",
    )(got, grad, accum.reshape(blocks, 1, block_rows), table)
    return new_table, new_accum.reshape(accum.shape)


def owner_partials(got, table, targets):
    slots = got.shape[0] * (got.shape[1] - 8)
    rows_dev, width = table.shape
    return pl.pallas_call(
        owner_kernel,
        out_shape=jax.ShapeDtypeStruct((targets, slots // targets, width), jnp.bfloat16),
        scratch_shapes=[pltpu.VMEM((slots, rows_dev), jnp.bfloat16)],
        compiler_params=pltpu.CompilerParams(vmem_limit_bytes=24 * 2**20),
        name="owner_partials",
    )(got, table)


def membership(codes, first_row, sums, proteins, per_p, slots):
    rows, lanes = codes.shape
    source = lax.broadcasted_iota(jnp.int32, (sums, rows), 0) // proteins + first_row
    spread = source == lax.broadcasted_iota(jnp.int32, (sums, rows), 1)
    by_row = jnp.dot(
        jnp.where(spread, 1.0, 0.0).astype(jnp.bfloat16),
        codes,
        preferred_element_type=jnp.float32,
    ).astype(jnp.bfloat16)
    slot = lax.broadcasted_iota(jnp.int32, (lanes, slots), 1)
    entry = (slot // per_p) * CAP + slot % CAP
    move = lax.broadcasted_iota(jnp.int32, (lanes, slots), 0) == entry
    code = jnp.dot(
        by_row, jnp.where(move, 1.0, 0.0).astype(jnp.bfloat16), preferred_element_type=jnp.float32
    ).astype(jnp.int32)
    row = lax.broadcasted_iota(jnp.int32, (sums, slots), 0)
    slot = lax.broadcasted_iota(jnp.int32, (sums, slots), 1)
    low = (row % proteins) * BLK_DEV
    mine = (row // proteins == (slot % per_p) // CAP) & (code > low) & (code <= low + BLK_DEV)
    return jnp.where(mine, 1.0, 0.0).astype(jnp.bfloat16)


def sum_kernel(codes_ref, got_ref, out_ref, member_ref):
    nz, proteins, _ = out_ref.shape
    _, per_p, width = got_ref.shape
    sums, slots = member_ref.shape
    codes = codes_ref[...].astype(jnp.float32)[:, 1, :].astype(jnp.bfloat16)
    member_ref[...] = membership(
        codes, lax.axis_index("zl") * nz, sums, proteins, per_p, slots
    )
    total = jnp.dot(
        member_ref[...], got_ref[...].reshape(slots, width), preferred_element_type=jnp.float32
    )
    out_ref[...] = total.reshape(out_ref.shape)


def protein_sums(codes, got, nz, proteins):
    npl, per_p, width = got.shape
    return pl.pallas_call(
        sum_kernel,
        out_shape=[
            jax.ShapeDtypeStruct((nz, proteins, width), jnp.float32),
            jax.ShapeDtypeStruct((nz * proteins, npl * per_p), jnp.bfloat16),
        ],
        compiler_params=pltpu.CompilerParams(vmem_limit_bytes=16 * 2**20),
        name="protein_sums",
    )(codes, got)


def select_kernel(member_ref, every_ref, out_ref):
    nz, rows, lanes = every_ref.shape
    width = out_ref.shape[2]
    proteins = rows * lanes // width
    every = every_ref[...].astype(jnp.float32)
    every = jnp.concatenate(
        [
            every[:, j : j + proteins, :].reshape(nz * proteins, lanes)
            for j in range(0, rows, proteins)
        ],
        axis=1,
    )
    picked = lax.dot_general(
        member_ref[...],
        every.astype(jnp.bfloat16),
        (((0,), (0,)), ((), ())),
        preferred_element_type=jnp.float32,
    )
    out_ref[...] = picked.astype(jnp.bfloat16).reshape(out_ref.shape)


def select_grads(member, every, npl, width):
    slots = member.shape[1]
    return pl.pallas_call(
        select_kernel,
        out_shape=jax.ShapeDtypeStruct((npl, slots // npl, width), jnp.bfloat16),
        compiler_params=pltpu.CompilerParams(vmem_limit_bytes=16 * 2**20),
        name="select_grads",
    )(member, every)


def exchange(x, axes):
    return lax.all_to_all(x, axes, split_axis=0, concat_axis=0, tiled=True)


def per_device(table, accum, pair_block, pair_protein, pair_weight, w_hidden, hidden_cot):
    nz, nl, nh = lax.axis_size("z"), lax.axis_size("zl"), lax.axis_size("xh")
    line, plane, group = nz * nl, lax.axis_size(PLANE), lax.axis_size(GROUP)
    block_rows = pair_weight.shape[1]
    proteins, width = hidden_cot.shape
    per_z = plane * CAP
    per_p = line * CAP

    first = route(pair_block, pair_protein, pair_weight, line, nl, nh, per_z, proteins)
    first = exchange(first, LINE)

    weights = first[:, :per_z].reshape(line, plane, CAP, block_rows).transpose(1, 0, 2, 3)
    codes = lax.optimization_barrier(first[:, per_z:])
    code = codes[:, 0, :per_z].astype(jnp.int32).reshape(line, plane, CAP).transpose(1, 0, 2)
    block = ((code - 1) & (BLK_DEV - 1)).astype(jnp.bfloat16).reshape(plane, 1, per_p)
    block = jnp.pad(block, ((0, 0), (0, 7), (0, block_rows - per_p)))
    second = exchange(
        jnp.concatenate([weights.reshape(plane, per_p, block_rows), block], axis=1), PLANE
    )
    partial_value = owner_partials(second, table, group)

    sums, member = protein_sums(codes, exchange(partial_value, GROUP), nz, proteins)
    dbag = dense_layer(exchange(sums, "z"), w_hidden, hidden_cot)

    every = exchange(dbag, "z")
    grad = exchange(select_grads(member, every, group, width), GROUP)
    return update_rows(second, grad, table, accum)


def solution(mesh):
    split = Mesh(mesh.devices.reshape(SIZES), AXES)
    in_specs = (
        P(AXES, None),
        P(AXES),
        P(AXES),
        P(AXES),
        P(AXES, None),
        P(),
        P(AXES, None),
    )
    out_specs = (P(AXES, None), P(AXES))
    return jax.shard_map(
        per_device, mesh=split, in_specs=in_specs, out_specs=out_specs, check_vma=False
    )
```

time: 171 us -> 169 us (0.988)
  blocking collectives: 161 us -> 158 us
    all_to_all x6, blocking collectives: 161 us -> 158 us  [exchange(): return lax.all_to_all(x, axes, split_axis=0, concat_axis=0, tiled=True)]
where the time goes in v5:
time: 169 us; the launch traced here: 168 us
  blocking collectives  158 us (93%)
  Pallas kernels  8.71 us (5%)
    all_to_all x6, blocking collectives, exchange(): return lax.all_to_all(x, axes, split_axis=0, concat_axis=0, tiled=True)  158 us

profile of v5, /device:TPU:1, one launch (start us, length us, event | category | flops | bytes accessed | tf_op | source)
XLA Modules:
  0.0 168.4 jit_solution(2883919815751031554)
XLA Ops:
  0.6 0.0 copy-start
  0.6 1.7 %route.1 = bf16[16,72,128]{2,1,0:T(8,128)(2,1)S(1)} custom-call(s32[1,512]{1,0:T(1,128)} %bitcast.17, s32[1,512]{1,0:T(1,128)} %bitcast.18, bf16[512,128]{1,0:T(8,128)(2,1)} %weight_in.1), custom_call_target="tpu_custom_call" | custom-call | tf_op jit(solution)/shard_map/route/pallas_call | solution.py:120
  2.4 29.6 %all_to_all.30 = bf16[16,72,128]{2,1,0:T(8,128)(2,1)S(1)} all-to-all(bf16[16,72,128]{2,1,0:T(8,128)(2,1)S(1)} %route.1), channel_id=1, replica_groups=mesh['xl'=2,'y'=4,'c'=2,'z'=8,'zl'=2,'xh'=2] {'zl','z'}, dimensions={0} | all-to-all | bytes 589824 | tf_op jit(solution)/shard_map/all_to_all | solution.py:319
  32.0 0.2 copy.15
  32.2 0.1 copy.16
  32.3 0.1 copy.17
  32.4 0.1 copy.18
  32.6 21.7 %all_to_all.31.got_ref = bf16[32,40,128]{2,1,0:T(8,128)(2,1)S(1)} all-to-all(bf16[32,40,128]{2,1,0:T(8,128)(2,1)S(1)} %fusion.1), channel_id=1, replica_groups=mesh['xl'=2,'y'=4,'c'=2,'z'=8,'zl'=2,'xh'=2] {'xl','y','c','xh'}, dimensions={0} | all-to-all | bytes 655360 | tf_op jit(solution)/shard_map/all_to_all | solution.py:319
  54.3 0.0 copy-done
  54.3 1.3 owner_partials.1
  55.6 34.5 %all_to_all.32.got_ref = bf16[64,16,1024]{2,1,0:T(8,128)(2,1)S(1)} all-to-all(bf16[64,16,1024]{2,1,0:T(8,128)(2,1)S(1)} %owner_partials.1), channel_id=1, replica_groups=mesh['xl'=2,'y'=4,'c'=2,'z'=8,'zl'=2,'xh'=2] {'xl','y','c','xh','zl'}, dimensions={0} | all-to-all | bytes 4194304 | tf_op jit(solution)/shard_map/all_to_all | solution.py:319
  90.2 0.0 copy-start.1
  90.2 0.0 copy-start.2
  90.2 0.7 protein_sums.1
  90.9 22.1 %all_to_all.33.sums_ref = f32[8,4,1024]{2,1,0:T(4,128)S(1)} all-to-all(f32[8,4,1024]{2,1,0:T(4,128)S(1)} %get-tuple-element.7), channel_id=1, replica_groups=mesh['xl'=2,'y'=4,'c'=2,'z'=8,'zl'=2,'xh'=2] {'z'}, dimensions={0} | all-to-all | bytes 262144 | tf_op jit(solution)/shard_map/all_to_all | solution.py:319
  113.0 0.0 copy-done.1
  113.0 0.0 copy-done.2
  113.0 1.1 dense_layer.1
  114.1 14.6 %all_to_all.34.every_ref = bf16[8,32,128]{2,1,0:T(8,128)(2,1)S(1)} all-to-all(bf16[8,32,128]{2,1,0:T(8,128)(2,1)S(1)} %dense_layer.1), channel_id=1, replica_groups=mesh['xl'=2,'y'=4,'c'=2,'z'=8,'zl'=2,'xh'=2] {'z'}, dimensions={0} | all-to-all | bytes 131072 | tf_op jit(solution)/shard_map/all_to_all | solution.py:319
  128.6 0.7 select_grads.1
  129.4 0.0 copy-start.3
  129.4 35.9 %all_to_all.35.grad_ref = bf16[64,16,1024]{2,1,0:T(8,128)(2,1)S(1)} all-to-all(bf16[64,16,1024]{2,1,0:T(8,128)(2,1)S(1)} %select_grads.1), channel_id=1, replica_groups=mesh['xl'=2,'y'=4,'c'=2,'z'=8,'zl'=2,'xh'=2] {'xl','y','c','xh','zl'}, dimensions={0} | all-to-all | bytes 4194304 | tf_op jit(solution)/shard_map/all_to_all | solution.py:319
  165.3 0.0 copy-done.3
  165.3 3.1 %update_rows.1 = (bf16[512,1024]{1,0:T(8,128)(2,1)}, f32[4,1,128]{2,1,0:T(1,128)}) custom-call(bf16[32,40,128]{2,1,0:T(8,128)(2,1)S(1)} %all_to_all.31.got_ref, bf16[64,16,1024]{2,1,0:T(8,128)(2,1)S(1)} %all_to_all.35.grad_ref, f32[4,1,128]{2,1,0:T(1,128)S(1)} %bitcast.12, bf16[512,1024]{1,0:T(8,128)(2,1)S(1)} %copy-done), custom_call_target="tpu_custom_call" | custom-call | tf_op jit(solution)/shard_map/update_rows/pallas_call | solution.py:210
  (4 shorter events, 0.1 us)
Async XLA Ops:
  0.6 53.6 %copy-start = (bf16[512,1024]{1,0:T(8,128)(2,1)S(1)}, bf16[512,1024]{1,0:T(8,128)(2,1)}, u32[]{:S(2)}) copy-start(bf16[512,1024]{1,0:T(8,128)(2,1)} %table_ref.3) | copy-start | bytes 3145732
  90.2 22.8 %copy-start.1 = (bf16[1024,1024]{1,0:T(8,128)(2,1)S(1)}, bf16[1024,1024]{1,0:T(8,128)(2,1)}, u32[]{:S(2)}) copy-start(bf16[1024,1024]{1,0:T(8,128)(2,1)} %w_ref.1) | copy-start | bytes 6291460
  90.2 22.8 %copy-start.2 = (bf16[4,1024]{1,0:T(4,128)(2,1)S(1)}, bf16[4,1024]{1,0:T(4,128)(2,1)}, u32[]{:S(2)}) copy-start(bf16[4,1024]{1,0:T(4,128)(2,1)} %cot_ref.1) | copy-start | bytes 24580
  129.4 35.9 %copy-start.3 = (f32[512]{0:T(512)S(1)}, f32[512]{0:T(512)}, u32[]{:S(2)}) copy-start(f32[512]{0:T(512)} %param.8) | copy-start | bytes 6148

commit v6 on v5

--- a/solution.py
+++ b/solution.py
@@ -165,24 +165,12 @@
     )
 
 
-def update_kernel(
-    got_ref,
-    grad_ref,
-    accum_ref,
-    table_ref,
-    table_out,
-    accum_out,
-    dense_ref,
-    sum_ref,
-):
-    slots = grad_ref.shape[0] * grad_ref.shape[1]
-    width = grad_ref.shape[2]
-    block_rows = got_ref.shape[2]
-    blocks = table_ref.shape[0] // block_rows
-    fill_dense(got_ref[...].astype(jnp.float32), got_ref.shape[1] - 8, dense_ref)
+def update_kernel(dense_ref, grad_ref, accum_ref, table_ref, table_out, accum_out, sum_ref):
+    slots = dense_ref.shape[0]
+    block_rows = accum_ref.shape[2]
     sum_ref[...] = lax.dot_general(
         dense_ref[...],
-        grad_ref[...].reshape(slots, width),
+        grad_ref[...].reshape(slots, grad_ref.shape[2]),
         (((0,), (0,)), ((), ())),
         preferred_element_type=jnp.float32,
     )
@@ -190,7 +178,7 @@
     diagonal = lax.broadcasted_iota(jnp.int32, square, 0) == lax.broadcasted_iota(
         jnp.int32, square, 1
     )
-    for b in range(blocks):
+    for b in range(accum_ref.shape[0]):
         rows = slice(b * block_rows, (b + 1) * block_rows)
         grad = sum_ref[rows, :]
         accum = jnp.sum(jnp.where(diagonal, accum_ref[b], 0.0), axis=1, keepdims=True)
@@ -202,10 +190,8 @@
         accum_out[b] = jnp.sum(jnp.where(diagonal, accum, 0.0), axis=0, keepdims=True)
 
 
-def update_rows(got, grad, table, accum):
-    block_rows = got.shape[2]
-    slots, width = grad.shape[0] * grad.shape[1], grad.shape[2]
-    rows_dev = table.shape[0]
+def update_rows(dense, grad, table, accum, block_rows):
+    rows_dev, width = table.shape
     blocks = rows_dev // block_rows
     new_table, new_accum = pl.pallas_call(
         update_kernel,
@@ -213,13 +199,10 @@
             jax.ShapeDtypeStruct(table.shape, table.dtype),
             jax.ShapeDtypeStruct((blocks, 1, block_rows), jnp.float32),
         ],
-        scratch_shapes=[
-            pltpu.VMEM((slots, rows_dev), jnp.bfloat16),
-            pltpu.VMEM((rows_dev, width), jnp.float32),
-        ],
+        scratch_shapes=[pltpu.VMEM((rows_dev, width), jnp.float32)],
         compiler_params=pltpu.CompilerParams(vmem_limit_bytes=24 * 2**20),
         name="update_rows",
-    )(got, grad, accum.reshape(blocks, 1, block_rows), table)
+    )(dense, grad, accum.reshape(blocks, 1, block_rows), table)
     return new_table, new_accum.reshape(accum.shape)
 
 
@@ -228,8 +211,10 @@
     rows_dev, width = table.shape
     return pl.pallas_call(
         owner_kernel,
-        out_shape=jax.ShapeDtypeStruct((targets, slots // targets, width), jnp.bfloat16),
-        scratch_shapes=[pltpu.VMEM((slots, rows_dev), jnp.bfloat16)],
+        out_shape=[
+            jax.ShapeDtypeStruct((targets, slots // targets, width), jnp.bfloat16),
+            jax.ShapeDtypeStruct((slots, rows_dev), jnp.bfloat16),
+        ],
         compiler_params=pltpu.CompilerParams(vmem_limit_bytes=24 * 2**20),
         name="owner_partials",
     )(got, table)
@@ -338,14 +323,14 @@
     second = exchange(
         jnp.concatenate([weights.reshape(plane, per_p, block_rows), block], axis=1), PLANE
     )
-    partial_value = owner_partials(second, table, group)
+    partial_value, dense = owner_partials(second, table, group)
 
     sums, member = protein_sums(codes, exchange(partial_value, GROUP), nz, proteins)
     dbag = dense_layer(exchange(sums, "z"), w_hidden, hidden_cot)
 
     every = exchange(dbag, "z")
     grad = exchange(select_grads(member, every, group, width), GROUP)
-    return update_rows(second, grad, table, accum)
+    return update_rows(dense, grad, table, accum, block_rows)
 
 
 def solution(mesh):

time: 169 us -> 169 us (level)
  no operation moved by 1% of the time
where the time goes in v6:
time: 169 us; the launch traced here: 168 us
  blocking collectives  159 us (94%)
  Pallas kernels  8.22 us (5%)
    all_to_all x6, blocking collectives, exchange(): return lax.all_to_all(x, axes, split_axis=0, concat_axis=0, tiled=True)  159 us

profile of v6, /device:TPU:1, one launch (start us, length us, event | category | flops | bytes accessed | tf_op | source)
XLA Modules:
  0.0 168.2 jit_solution(3893788752270913968)
XLA Ops:
  0.6 0.0 copy-start
  0.6 1.7 %route.1 = bf16[16,72,128]{2,1,0:T(8,128)(2,1)S(1)} custom-call(s32[1,512]{1,0:T(1,128)} %bitcast.17, s32[1,512]{1,0:T(1,128)} %bitcast.18, bf16[512,128]{1,0:T(8,128)(2,1)} %weight_in.1), custom_call_target="tpu_custom_call" | custom-call | tf_op jit(solution)/shard_map/route/pallas_call | solution.py:120
  2.4 29.6 %all_to_all.30 = bf16[16,72,128]{2,1,0:T(8,128)(2,1)S(1)} all-to-all(bf16[16,72,128]{2,1,0:T(8,128)(2,1)S(1)} %route.1), channel_id=1, replica_groups=mesh['xl'=2,'y'=4,'c'=2,'z'=8,'zl'=2,'xh'=2] {'zl','z'}, dimensions={0} | all-to-all | bytes 589824 | tf_op jit(solution)/shard_map/all_to_all | solution.py:304
  32.0 0.2 copy.15
  32.2 0.1 copy.16
  32.3 0.1 copy.17
  32.4 0.1 copy.18
  32.6 21.7 %all_to_all.31.got_ref = bf16[32,40,128]{2,1,0:T(8,128)(2,1)S(1)} all-to-all(bf16[32,40,128]{2,1,0:T(8,128)(2,1)S(1)} %fusion.1), channel_id=1, replica_groups=mesh['xl'=2,'y'=4,'c'=2,'z'=8,'zl'=2,'xh'=2] {'xl','y','c','xh'}, dimensions={0} | all-to-all | bytes 655360 | tf_op jit(solution)/shard_map/all_to_all | solution.py:304
  54.3 0.0 copy-done
  54.3 1.3 owner_partials.1
  55.6 34.5 %all_to_all.32.got_ref = bf16[64,16,1024]{2,1,0:T(8,128)(2,1)S(1)} all-to-all(bf16[64,16,1024]{2,1,0:T(8,128)(2,1)S(1)} %get-tuple-element.9), channel_id=1, replica_groups=mesh['xl'=2,'y'=4,'c'=2,'z'=8,'zl'=2,'xh'=2] {'xl','y','c','xh','zl'}, dimensions={0} | all-to-all | bytes 4194304 | tf_op jit(solution)/shard_map/all_to_all | solution.py:304
  90.2 0.0 copy-start.1
  90.2 0.0 copy-start.2
  90.2 0.7 protein_sums.1
  90.9 22.1 %all_to_all.33.sums_ref = f32[8,4,1024]{2,1,0:T(4,128)S(1)} all-to-all(f32[8,4,1024]{2,1,0:T(4,128)S(1)} %get-tuple-element.11), channel_id=1, replica_groups=mesh['xl'=2,'y'=4,'c'=2,'z'=8,'zl'=2,'xh'=2] {'z'}, dimensions={0} | all-to-all | bytes 262144 | tf_op jit(solution)/shard_map/all_to_all | solution.py:304
  113.0 0.0 copy-done.1
  113.0 0.0 copy-done.2
  113.0 1.1 dense_layer.1
  114.1 14.6 %all_to_all.34.every_ref = bf16[8,32,128]{2,1,0:T(8,128)(2,1)S(1)} all-to-all(bf16[8,32,128]{2,1,0:T(8,128)(2,1)S(1)} %dense_layer.1), channel_id=1, replica_groups=mesh['xl'=2,'y'=4,'c'=2,'z'=8,'zl'=2,'xh'=2] {'z'}, dimensions={0} | all-to-all | bytes 131072 | tf_op jit(solution)/shard_map/all_to_all | solution.py:304
  128.7 0.7 select_grads.1
  129.4 0.0 copy-start.3
  129.4 36.2 %all_to_all.35.grad_ref = bf16[64,16,1024]{2,1,0:T(8,128)(2,1)S(1)} all-to-all(bf16[64,16,1024]{2,1,0:T(8,128)(2,1)S(1)} %select_grads.1), channel_id=1, replica_groups=mesh['xl'=2,'y'=4,'c'=2,'z'=8,'zl'=2,'xh'=2] {'xl','y','c','xh','zl'}, dimensions={0} | all-to-all | bytes 4194304 | tf_op jit(solution)/shard_map/all_to_all | solution.py:304
  165.6 0.0 copy-done.3
  165.6 2.6 %update_rows.1 = (bf16[512,1024]{1,0:T(8,128)(2,1)}, f32[4,1,128]{2,1,0:T(1,128)}) custom-call(bf16[1024,512]{1,0:T(8,128)(2,1)S(1)} %get-tuple-element.8.dense_ref, bf16[64,16,1024]{2,1,0:T(8,128)(2,1)S(1)} %all_to_all.35.grad_ref, f32[4,1,128]{2,1,0:T(1,128)S(1)} %bitcast.12, bf16[512,1024]{1,0:T(8,128)(2,1)S(1)} %copy-done), custom_call_target="tpu_custom_call" | custom-call | tf_op jit(solution)/shard_map/update_rows/pallas_call | solution.py:196
  (4 shorter events, 0.1 us)
Async XLA Ops:
  0.6 53.6 %copy-start = (bf16[512,1024]{1,0:T(8,128)(2,1)S(1)}, bf16[512,1024]{1,0:T(8,128)(2,1)}, u32[]{:S(2)}) copy-start(bf16[512,1024]{1,0:T(8,128)(2,1)} %table_ref.3) | copy-start | bytes 3145732
  90.2 22.8 %copy-start.1 = (bf16[1024,1024]{1,0:T(8,128)(2,1)S(1)}, bf16[1024,1024]{1,0:T(8,128)(2,1)}, u32[]{:S(2)}) copy-start(bf16[1024,1024]{1,0:T(8,128)(2,1)} %w_ref.1) | copy-start | bytes 6291460
  90.2 22.8 %copy-start.2 = (bf16[4,1024]{1,0:T(4,128)(2,1)S(1)}, bf16[4,1024]{1,0:T(4,128)(2,1)}, u32[]{:S(2)}) copy-start(bf16[4,1024]{1,0:T(4,128)(2,1)} %cot_ref.1) | copy-start | bytes 24580
  129.4 36.2 %copy-start.3 = (f32[512]{0:T(512)S(1)}, f32[512]{0:T(512)}, u32[]{:S(2)}) copy-start(f32[512]{0:T(512)} %param.8) | copy-start | bytes 6148

commit v7 on v6

--- a/solution.py
+++ b/solution.py
@@ -62,9 +62,9 @@
         copy.start()
     for copy in copies:
         copy.wait()
-    line, rows, block_rows = out_ref.shape
+    line, groups, _, block_rows = out_ref.shape
     pairs = block_ref.shape[1]
-    per_z = rows - 8
+    per_z = (groups - 1) * CAP
     slots = line * per_z
     block = block_ref[...]
     owner = block // BLK_DEV
@@ -105,11 +105,12 @@
     own = code_rows(zl * nz + z, line, plane * CAP + rank)
     both = code_rows(z, nz, (plane * nl + zl) * CAP + rank)
     both = jnp.concatenate([both] * nl, axis=0)
-    row = lax.broadcasted_iota(jnp.int32, (line, 8, block_rows), 1)
+    row = lax.broadcasted_iota(jnp.int32, (line, 1, CAP, block_rows), 2)
+    own, both = own[:, None, None, :], both[:, None, None, :]
     out_ref[...] = jnp.concatenate(
         [
-            send.reshape(line, per_z, block_rows),
-            jnp.where(row == 0, own[:, None, :], both[:, None, :]),
+            send.reshape(line, groups - 1, CAP, block_rows),
+            jnp.where(row == 0, own, both),
         ],
         axis=1,
     ).astype(jnp.bfloat16)
@@ -120,7 +121,7 @@
     return pl.pallas_call(
         functools.partial(route_kernel, nl, nh, proteins),
         in_specs=[pl.BlockSpec(memory_space=pl.ANY)] * 3,
-        out_shape=jax.ShapeDtypeStruct((line, per_z + 8, block_rows), jnp.bfloat16),
+        out_shape=jax.ShapeDtypeStruct((line, per_z // CAP + 1, CAP, block_rows), jnp.bfloat16),
         scratch_shapes=[
             pltpu.VMEM((1, pairs), jnp.int32),
             pltpu.VMEM((1, pairs), jnp.int32),
@@ -136,28 +137,22 @@
     )
 
 
-def slot_blocks(got, per_p):
-    shape = (got.shape[0], per_p, got.shape[2])
+def owner_kernel(got_ref, table_ref, partial_ref, dense_ref):
+    places, groups, _, block_rows = got_ref.shape
+    per_p = (groups - 1) * CAP
+    got = got_ref[...].astype(jnp.float32)
+    weights = got[:, : groups - 1].reshape(places, per_p, block_rows)
+    shape = (places, per_p, block_rows)
     diagonal = lax.broadcasted_iota(jnp.int32, shape, 1) == lax.broadcasted_iota(
         jnp.int32, shape, 2
     )
-    row = got[:, per_p : per_p + 1, :]
-    return jnp.sum(jnp.where(diagonal, row, 0.0), axis=2, keepdims=True)
-
-
-def fill_dense(got, per_p, dense_ref):
-    groups, _, block_rows = got.shape
-    block = slot_blocks(got, per_p)
-    weights = got[:, :per_p, :]
+    row = got[:, groups - 1, :1, :]
+    block = jnp.sum(jnp.where(diagonal, row, 0.0), axis=2, keepdims=True)
     for b in range(dense_ref.shape[1] // block_rows):
         mine = jnp.where(block == b, weights, 0.0).astype(jnp.bfloat16)
         dense_ref[:, b * block_rows : (b + 1) * block_rows] = mine.reshape(
-            groups * per_p, block_rows
+            places * per_p, block_rows
         )
-
-
-def owner_kernel(got_ref, table_ref, partial_ref, dense_ref):
-    fill_dense(got_ref[...].astype(jnp.float32), got_ref.shape[1] - 8, dense_ref)
     partial_ref[...] = (
         jnp.dot(dense_ref[...], table_ref[...], preferred_element_type=jnp.float32)
         .astype(jnp.bfloat16)
@@ -207,7 +202,7 @@
 
 
 def owner_partials(got, table, targets):
-    slots = got.shape[0] * (got.shape[1] - 8)
+    slots = got.shape[0] * (got.shape[1] - 1) * CAP
     rows_dev, width = table.shape
     return pl.pallas_call(
         owner_kernel,
@@ -315,14 +310,12 @@
     first = route(pair_block, pair_protein, pair_weight, line, nl, nh, per_z, proteins)
     first = exchange(first, LINE)
 
-    weights = first[:, :per_z].reshape(line, plane, CAP, block_rows).transpose(1, 0, 2, 3)
-    codes = lax.optimization_barrier(first[:, per_z:])
+    weights = first[:, :plane].transpose(1, 0, 2, 3)
+    codes = lax.optimization_barrier(first[:, plane])
     code = codes[:, 0, :per_z].astype(jnp.int32).reshape(line, plane, CAP).transpose(1, 0, 2)
-    block = ((code - 1) & (BLK_DEV - 1)).astype(jnp.bfloat16).reshape(plane, 1, per_p)
-    block = jnp.pad(block, ((0, 0), (0, 7), (0, block_rows - per_p)))
-    second = exchange(
-        jnp.concatenate([weights.reshape(plane, per_p, block_rows), block], axis=1), PLANE
-    )
+    block = ((code - 1) & (BLK_DEV - 1)).astype(jnp.bfloat16).reshape(plane, 1, 1, per_p)
+    block = jnp.pad(block, ((0, 0), (0, 0), (0, CAP - 1), (0, block_rows - per_p)))
+    second = exchange(jnp.concatenate([weights, block], axis=1), PLANE)
     partial_value, dense = owner_partials(second, table, group)
 
     sums, member = protein_sums(codes, exchange(partial_value, GROUP), nz, proteins)

time: 169 us -> 167 us (0.988)
  blocking collectives: 159 us -> 157 us
    all_to_all x6, blocking collectives: 159 us -> 157 us  [exchange(): return lax.all_to_all(x, axes, split_axis=0, concat_axis=0, tiled=True)]
where the time goes in v7:
time: 167 us
  blocking collectives  157 us (94%)
  Pallas kernels  8.34 us (5%)
    all_to_all x6, blocking collectives, exchange(): return lax.all_to_all(x, axes, split_axis=0, concat_axis=0, tiled=True)  157 us

profile of v7, /device:TPU:1, one launch (start us, length us, event | category | flops | bytes accessed | tf_op | source)
XLA Modules:
  0.0 166.7 jit_solution(3677887718347514592)
XLA Ops:
  0.6 0.0 copy-start
  0.6 1.7 %route.1 = bf16[16,33,2,128]{3,2,1,0:T(2,128)(2,1)S(1)} custom-call(s32[1,512]{1,0:T(1,128)} %bitcast.17, s32[1,512]{1,0:T(1,128)} %bitcast.18, bf16[512,128]{1,0:T(8,128)(2,1)} %weight_in.1), custom_call_target="tpu_custom_call" | custom-call | tf_op jit(solution)/shard_map/route/pallas_call | solution.py:121
  2.4 29.3 %all_to_all.30 = bf16[16,33,2,128]{3,2,1,0:T(2,128)(2,1)S(1)} all-to-all(bf16[16,33,2,128]{3,2,1,0:T(2,128)(2,1)S(1)} %route.1), channel_id=1, replica_groups=mesh['xl'=2,'y'=4,'c'=2,'z'=8,'zl'=2,'xh'=2] {'zl','z'}, dimensions={0} | all-to-all | bytes 540672 | tf_op jit(solution)/shard_map/all_to_all | solution.py:299
  31.7 0.1 copy.22
  31.8 0.1 copy.23
  31.9 0.1 copy.24
  32.0 0.2 copy_bitcast_fusion
  32.2 0.3 fusion
  32.5 20.9 %all_to_all.31.got_ref = bf16[32,17,2,128]{3,2,1,0:T(2,128)(2,1)S(1)} all-to-all(bf16[32,17,2,128]{3,2,1,0:T(2,128)(2,1)S(1)} %fusion), channel_id=1, replica_groups=mesh['xl'=2,'y'=4,'c'=2,'z'=8,'zl'=2,'xh'=2] {'xl','y','c','xh'}, dimensions={0} | all-to-all | bytes 557056 | tf_op jit(solution)/shard_map/all_to_all | solution.py:299
  53.4 0.0 copy-done
  53.4 1.4 owner_partials.1
  54.9 34.2 %all_to_all.32.got_ref = bf16[64,16,1024]{2,1,0:T(8,128)(2,1)S(1)} all-to-all(bf16[64,16,1024]{2,1,0:T(8,128)(2,1)S(1)} %get-tuple-element.9), channel_id=1, replica_groups=mesh['xl'=2,'y'=4,'c'=2,'z'=8,'zl'=2,'xh'=2] {'xl','y','c','xh','zl'}, dimensions={0} | all-to-all | bytes 4194304 | tf_op jit(solution)/shard_map/all_to_all | solution.py:299
  89.1 0.0 copy-start.1
  89.1 0.0 copy-start.2
  89.1 0.7 protein_sums.1
  89.8 21.9 %all_to_all.33.sums_ref = f32[8,4,1024]{2,1,0:T(4,128)S(1)} all-to-all(f32[8,4,1024]{2,1,0:T(4,128)S(1)} %get-tuple-element.11), channel_id=1, replica_groups=mesh['xl'=2,'y'=4,'c'=2,'z'=8,'zl'=2,'xh'=2] {'z'}, dimensions={0} | all-to-all | bytes 262144 | tf_op jit(solution)/shard_map/all_to_all | solution.py:299
  111.7 0.0 copy-done.1
  111.7 0.0 copy-done.2
  111.7 1.1 dense_layer.1
  112.8 14.6 %all_to_all.34.every_ref = bf16[8,32,128]{2,1,0:T(8,128)(2,1)S(1)} all-to-all(bf16[8,32,128]{2,1,0:T(8,128)(2,1)S(1)} %dense_layer.1), channel_id=1, replica_groups=mesh['xl'=2,'y'=4,'c'=2,'z'=8,'zl'=2,'xh'=2] {'z'}, dimensions={0} | all-to-all | bytes 131072 | tf_op jit(solution)/shard_map/all_to_all | solution.py:299
  127.4 0.7 select_grads.1
  128.1 0.0 copy-start.3
  128.2 35.9 %all_to_all.35.grad_ref = bf16[64,16,1024]{2,1,0:T(8,128)(2,1)S(1)} all-to-all(bf16[64,16,1024]{2,1,0:T(8,128)(2,1)S(1)} %select_grads.1), channel_id=1, replica_groups=mesh['xl'=2,'y'=4,'c'=2,'z'=8,'zl'=2,'xh'=2] {'xl','y','c','xh','zl'}, dimensions={0} | all-to-all | bytes 4194304 | tf_op jit(solution)/shard_map/all_to_all | solution.py:299
  164.1 0.0 copy-done.3
  164.1 2.6 %update_rows.1 = (bf16[512,1024]{1,0:T(8,128)(2,1)}, f32[4,1,128]{2,1,0:T(1,128)}) custom-call(bf16[1024,512]{1,0:T(8,128)(2,1)S(1)} %get-tuple-element.8.dense_ref, bf16[64,16,1024]{2,1,0:T(8,128)(2,1)S(1)} %all_to_all.35.grad_ref, f32[4,1,128]{2,1,0:T(1,128)S(1)} %bitcast.14, bf16[512,1024]{1,0:T(8,128)(2,1)S(1)} %copy-done), custom_call_target="tpu_custom_call" | custom-call | tf_op jit(solution)/shard_map/update_rows/pallas_call | solution.py:191
  (2 shorter events, 0.0 us)
Async XLA Ops:
  0.6 52.8 %copy-start = (bf16[512,1024]{1,0:T(8,128)(2,1)S(1)}, bf16[512,1024]{1,0:T(8,128)(2,1)}, u32[]{:S(2)}) copy-start(bf16[512,1024]{1,0:T(8,128)(2,1)} %table_ref.3) | copy-start | bytes 3145732
  89.1 22.6 %copy-start.1 = (bf16[1024,1024]{1,0:T(8,128)(2,1)S(1)}, bf16[1024,1024]{1,0:T(8,128)(2,1)}, u32[]{:S(2)}) copy-start(bf16[1024,1024]{1,0:T(8,128)(2,1)} %w_ref.1) | copy-start | bytes 6291460
  89.1 22.6 %copy-start.2 = (bf16[4,1024]{1,0:T(4,128)(2,1)S(1)}, bf16[4,1024]{1,0:T(4,128)(2,1)}, u32[]{:S(2)}) copy-start(bf16[4,1024]{1,0:T(4,128)(2,1)} %cot_ref.1) | copy-start | bytes 24580
  128.1 35.9 %copy-start.3 = (f32[512]{0:T(512)S(1)}, f32[512]{0:T(512)}, u32[]{:S(2)}) copy-start(f32[512]{0:T(512)} %param.8) | copy-start | bytes 6148

commit v8 on v7

--- a/solution.py
+++ b/solution.py
@@ -135,6 +135,44 @@
         pltpu.with_memory_space_constraint(pair_protein.reshape(1, pairs), pltpu.HBM),
         pltpu.with_memory_space_constraint(pair_weight, pltpu.HBM),
     )
+
+
+def forward_kernel(first_ref, out_ref):
+    line, groups, _, lanes = first_ref.shape
+    plane = groups - 1
+    for z in range(line):
+        out_ref[:, z] = first_ref[z, :plane]
+    code = first_ref[:, plane].astype(jnp.float32)[:, 0, :].astype(jnp.int32)
+    block = ((code - 1) & (BLK_DEV - 1)).astype(jnp.float32).astype(jnp.bfloat16)
+    rows = jnp.zeros((plane, lanes), jnp.float32)
+    for r in range(CAP):
+        pick = lax.broadcasted_iota(jnp.int32, (lanes, plane), 0) == (
+            lax.broadcasted_iota(jnp.int32, (lanes, plane), 1) * CAP + r
+        )
+        put = lax.broadcasted_iota(jnp.int32, (line, lanes), 1) == (
+            lax.broadcasted_iota(jnp.int32, (line, lanes), 0) * CAP + r
+        )
+        picked = jnp.dot(
+            block, jnp.where(pick, 1.0, 0.0).astype(jnp.bfloat16), preferred_element_type=jnp.float32
+        )
+        rows = rows + lax.dot_general(
+            picked.astype(jnp.bfloat16),
+            jnp.where(put, 1.0, 0.0).astype(jnp.bfloat16),
+            (((0,), (0,)), ((), ())),
+            preferred_element_type=jnp.float32,
+        )
+    row = lax.broadcasted_iota(jnp.int32, (plane, CAP, lanes), 1)
+    out_ref[:, line] = jnp.where(row == 0, rows[:, None, :], 0.0).astype(jnp.bfloat16)
+
+
+def forward(first):
+    line, groups, cap, lanes = first.shape
+    return pl.pallas_call(
+        forward_kernel,
+        out_shape=jax.ShapeDtypeStruct((groups - 1, line + 1, cap, lanes), first.dtype),
+        compiler_params=pltpu.CompilerParams(vmem_limit_bytes=16 * 2**20),
+        name="forward",
+    )(first)
 
 
 def owner_kernel(got_ref, table_ref, partial_ref, dense_ref):
@@ -237,11 +275,12 @@
     return jnp.where(mine, 1.0, 0.0).astype(jnp.bfloat16)
 
 
-def sum_kernel(codes_ref, got_ref, out_ref, member_ref):
+def sum_kernel(first_ref, got_ref, out_ref, member_ref):
     nz, proteins, _ = out_ref.shape
     _, per_p, width = got_ref.shape
     sums, slots = member_ref.shape
-    codes = codes_ref[...].astype(jnp.float32)[:, 1, :].astype(jnp.bfloat16)
+    codes = first_ref[:, first_ref.shape[1] - 1].astype(jnp.float32)[:, 1, :]
+    codes = codes.astype(jnp.bfloat16)
     member_ref[...] = membership(
         codes, lax.axis_index("zl") * nz, sums, proteins, per_p, slots
     )
@@ -251,7 +290,7 @@
     out_ref[...] = total.reshape(out_ref.shape)
 
 
-def protein_sums(codes, got, nz, proteins):
+def protein_sums(first, got, nz, proteins):
     npl, per_p, width = got.shape
     return pl.pallas_call(
         sum_kernel,
@@ -261,7 +300,7 @@
         ],
         compiler_params=pltpu.CompilerParams(vmem_limit_bytes=16 * 2**20),
         name="protein_sums",
-    )(codes, got)
+    )(first, got)
 
 
 def select_kernel(member_ref, every_ref, out_ref):
@@ -305,20 +344,14 @@
     block_rows = pair_weight.shape[1]
     proteins, width = hidden_cot.shape
     per_z = plane * CAP
-    per_p = line * CAP
 
     first = route(pair_block, pair_protein, pair_weight, line, nl, nh, per_z, proteins)
     first = exchange(first, LINE)
 
-    weights = first[:, :plane].transpose(1, 0, 2, 3)
-    codes = lax.optimization_barrier(first[:, plane])
-    code = codes[:, 0, :per_z].astype(jnp.int32).reshape(line, plane, CAP).transpose(1, 0, 2)
-    block = ((code - 1) & (BLK_DEV - 1)).astype(jnp.bfloat16).reshape(plane, 1, 1, per_p)
-    block = jnp.pad(block, ((0, 0), (0, 0), (0, CAP - 1), (0, block_rows - per_p)))
-    second = exchange(jnp.concatenate([weights, block], axis=1), PLANE)
+    second = exchange(forward(first), PLANE)
     partial_value, dense = owner_partials(second, table, group)
 
-    sums, member = protein_sums(codes, exchange(partial_value, GROUP), nz, proteins)
+    sums, member = protein_sums(first, exchange(partial_value, GROUP), nz, proteins)
     dbag = dense_layer(exchange(sums, "z"), w_hidden, hidden_cot)
 
     every = exchange(dbag, "z")

time: 167 us -> 167 us (level)
  no operation moved by 1% of the time
where the time goes in v8:
time: 167 us; the launch traced here: 166 us
  blocking collectives  157 us (94%)
  Pallas kernels  8.82 us (5%)
    all_to_all x6, blocking collectives, exchange(): return lax.all_to_all(x, axes, split_axis=0, concat_axis=0, tiled=True)  157 us

profile of v8, /device:TPU:1, one launch (start us, length us, event | category | flops | bytes accessed | tf_op | source)
XLA Modules:
  0.0 166.4 jit_solution(9485781034946613759)
XLA Ops:
  0.6 0.0 copy-start
  0.6 1.7 %route.1 = bf16[16,33,2,128]{3,2,1,0:T(2,128)(2,1)S(1)} custom-call(s32[1,512]{1,0:T(1,128)} %bitcast.5, s32[1,512]{1,0:T(1,128)} %bitcast.6, bf16[512,128]{1,0:T(8,128)(2,1)} %weight_in.1), custom_call_target="tpu_custom_call" | custom-call | tf_op jit(solution)/shard_map/route/pallas_call | solution.py:121
  2.4 29.3 %all_to_all.30.first_ref = bf16[16,33,2,128]{3,2,1,0:T(2,128)(2,1)S(1)} all-to-all(bf16[16,33,2,128]{3,2,1,0:T(2,128)(2,1)S(1)} %route.1), channel_id=1, replica_groups=mesh['xl'=2,'y'=4,'c'=2,'z'=8,'zl'=2,'xh'=2] {'zl','z'}, dimensions={0} | all-to-all | bytes 540672 | tf_op jit(solution)/shard_map/all_to_all | solution.py:338
  31.7 0.5 forward.1
  32.2 20.9 %all_to_all.31.got_ref = bf16[32,17,2,128]{3,2,1,0:T(2,128)(2,1)S(1)} all-to-all(bf16[32,17,2,128]{3,2,1,0:T(2,128)(2,1)S(1)} %forward.1), channel_id=1, replica_groups=mesh['xl'=2,'y'=4,'c'=2,'z'=8,'zl'=2,'xh'=2] {'xl','y','c','xh'}, dimensions={0} | all-to-all | bytes 557056 | tf_op jit(solution)/shard_map/all_to_all | solution.py:338
  53.1 0.0 copy-done
  53.1 1.4 owner_partials.1
  54.6 34.3 %all_to_all.32.got_ref = bf16[64,16,1024]{2,1,0:T(8,128)(2,1)S(1)} all-to-all(bf16[64,16,1024]{2,1,0:T(8,128)(2,1)S(1)} %get-tuple-element.9), channel_id=1, replica_groups=mesh['xl'=2,'y'=4,'c'=2,'z'=8,'zl'=2,'xh'=2] {'xl','y','c','xh','zl'}, dimensions={0} | all-to-all | bytes 4194304 | tf_op jit(solution)/shard_map/all_to_all | solution.py:338
  88.8 0.0 copy-start.1
  88.8 0.0 copy-start.2
  88.8 0.7 protein_sums.1
  89.6 21.9 %all_to_all.33.sums_ref = f32[8,4,1024]{2,1,0:T(4,128)S(1)} all-to-all(f32[8,4,1024]{2,1,0:T(4,128)S(1)} %get-tuple-element.11), channel_id=1, replica_groups=mesh['xl'=2,'y'=4,'c'=2,'z'=8,'zl'=2,'xh'=2] {'z'}, dimensions={0} | all-to-all | bytes 262144 | tf_op jit(solution)/shard_map/all_to_all | solution.py:338
  111.5 0.0 copy-done.1
  111.5 0.0 copy-done.2
  111.5 1.1 dense_layer.1
  112.6 14.6 %all_to_all.34.every_ref = bf16[8,32,128]{2,1,0:T(8,128)(2,1)S(1)} all-to-all(bf16[8,32,128]{2,1,0:T(8,128)(2,1)S(1)} %dense_layer.1), channel_id=1, replica_groups=mesh['xl'=2,'y'=4,'c'=2,'z'=8,'zl'=2,'xh'=2] {'z'}, dimensions={0} | all-to-all | bytes 131072 | tf_op jit(solution)/shard_map/all_to_all | solution.py:338
  127.1 0.7 select_grads.1
  127.9 0.0 copy-start.3
  127.9 35.9 %all_to_all.35.grad_ref = bf16[64,16,1024]{2,1,0:T(8,128)(2,1)S(1)} all-to-all(bf16[64,16,1024]{2,1,0:T(8,128)(2,1)S(1)} %select_grads.1), channel_id=1, replica_groups=mesh['xl'=2,'y'=4,'c'=2,'z'=8,'zl'=2,'xh'=2] {'xl','y','c','xh','zl'}, dimensions={0} | all-to-all | bytes 4194304 | tf_op jit(solution)/shard_map/all_to_all | solution.py:338
  163.8 0.0 copy-done.3
  163.8 2.6 %update_rows.1 = (bf16[512,1024]{1,0:T(8,128)(2,1)}, f32[4,1,128]{2,1,0:T(1,128)}) custom-call(bf16[1024,512]{1,0:T(8,128)(2,1)S(1)} %get-tuple-element.8.dense_ref, bf16[64,16,1024]{2,1,0:T(8,128)(2,1)S(1)} %all_to_all.35.grad_ref, f32[4,1,128]{2,1,0:T(1,128)S(1)} %bitcast.4, bf16[512,1024]{1,0:T(8,128)(2,1)S(1)} %copy-done), custom_call_target="tpu_custom_call" | custom-call | tf_op jit(solution)/shard_map/update_rows/pallas_call | solution.py:229
Async XLA Ops:
  0.6 52.5 %copy-start = (bf16[512,1024]{1,0:T(8,128)(2,1)S(1)}, bf16[512,1024]{1,0:T(8,128)(2,1)}, u32[]{:S(2)}) copy-start(bf16[512,1024]{1,0:T(8,128)(2,1)} %table_ref.3) | copy-start | bytes 3145732
  88.8 22.6 %copy-start.1 = (bf16[1024,1024]{1,0:T(8,128)(2,1)S(1)}, bf16[1024,1024]{1,0:T(8,128)(2,1)}, u32[]{:S(2)}) copy-start(bf16[1024,1024]{1,0:T(8,128)(2,1)} %w_ref.1) | copy-start | bytes 6291460
  88.8 22.6 %copy-start.2 = (bf16[4,1024]{1,0:T(4,128)(2,1)S(1)}, bf16[4,1024]{1,0:T(4,128)(2,1)}, u32[]{:S(2)}) copy-start(bf16[4,1024]{1,0:T(4,128)(2,1)} %cot_ref.1) | copy-start | bytes 24580
  127.9 35.9 %copy-start.3 = (f32[512]{0:T(512)S(1)}, f32[512]{0:T(512)}, u32[]{:S(2)}) copy-start(f32[512]{0:T(512)} %param.8) | copy-start | bytes 6148
